TPU v7x, 128 devices: a whole 4x4x4 slice. The times are simulated.
128 devices in a mesh: sample: 4 (over z_hi, core), row: 32 (over x, z_lo, y).
Axes of the slice: x: 4, y: 4, z: 4 (z_hi: 2, z_lo: 2; z = z_hi * 2 + z_lo), core: 2. Of those that a mesh axis runs over, the one named last changes fastest.
Arguments:
- fine_state: float32 [8, 512, 16384], P('sample', 'row'), parts along dimension 0, may hold values from -3 to 3
- noise: bfloat16 [12, 2, 512, 16384], P('sample', None, 'row'), parts along dimension 0, may hold values from -6 to 6
Outputs:
- fine_final: float32 [8, 512, 16384], P('sample', 'row'), parts along dimension 0
- coarse_final: float32 [8, 128, 4096], P('sample', 'row'), parts along dimension 0
- correction: float32 [8, 512, 16384], P('sample', 'row'), parts along dimension 0
There are 4 independent parts, one for each index of `sample`. A program takes and returns all parts, laid end to end along the dimension named above; each array names one. Nothing has to cross between parts.
All inputs are finite; a program needn't handle non-finite values.
Results may differ from a plain program's by a relative error of at most 0.0003.
Values sent between devices are 32-bit elements; how exact they have to be, the bound alone decides.
No kernel may reach another device: no remote copies, remote signals or barrier semaphores. Data moves between devices by JAX's collectives and lax.ppermute only.
A program may use at most 192 MiB of HBM per device.

v0:
```python
import functools

import jax
import jax.numpy as jnp
from jax import lax
from jax.experimental import pallas as pl
from jax.experimental.pallas import tpu as pltpu
from jax.sharding import PartitionSpec as P

NEAR, FAR = 4.0 / 3.0, -1.0 / 12.0
DIFFUSE = (0.15, 0.05)
MIB = 1 << 20


def iota(dim):
    return lax.broadcasted_iota(jnp.int32, (8, 128), dim)


def pick(x, index):
    return jnp.take_along_axis(x, index, axis=0, mode="promise_in_bounds")


def turn(x, steps):
    return pltpu.roll(x, steps, 0)


def sideways(mid, left, right, lane):
    near = pltpu.roll(jnp.where(lane == 127, left, mid), 1, 1) + pltpu.roll(
        jnp.where(lane == 0, right, mid), 127, 1
    )
    far = pltpu.roll(jnp.where(lane >= 126, left, mid), 2, 1) + pltpu.roll(
        jnp.where(lane < 2, right, mid), 126, 1
    )
    return near, far


def stepped(a, b, near, far, force, scale, react):
    da, db = DIFFUSE[0] * scale, DIFFUSE[1] * scale
    new_a = a * ((1.0 + react - 5.0 * da) - (react / 3.0) * (a * a)) - react * b
    new_a = new_a + (da * NEAR) * near[0] + (da * FAR) * far[0] + force[0]
    low = 0.08 * react
    new_b = b * (1.0 - 5.0 * db - 0.8 * low) + low * a + 0.7 * low
    new_b = new_b + (db * NEAR) * near[1] + (db * FAR) * far[1] + force[1]
    return new_a, new_b


def both_ends(ref, which, first, sub):
    block = which.astype(jnp.float32)
    half = sub >> 1
    top = pick(block[0:8], half + first)
    low = pick(block[8:16], 7 - first - half)
    return jnp.where((sub & 1) == 0, top, low)


def pre_kernel(row_axis, f_hbm, n_hbm, m_odd, m_even, x0, f1, own, own_q, fbuf, nbuf, sems):
    nb = x0.shape[1] - 2
    chunks = 4
    width = nb // chunks
    copies = []
    for c in range(chunks):
        cols = pl.ds(c * width * 128, width * 128)
        copies.append(
            (
                pltpu.make_async_copy(f_hbm.at[:, :, cols], fbuf.at[:, :, cols], sems.at[0, c]),
                pltpu.make_async_copy(
                    n_hbm.at[0:2, :, :, cols], nbuf.at[:, :, :, cols], sems.at[1, c]
                ),
            )
        )
        copies[-1][0].start()
        copies[-1][1].start()
    sub, lane = iota(0), iota(1)
    parity = lax.rem(lax.axis_index(row_axis), 2)
    zero = jnp.zeros((8, 128), jnp.float32)
    for f in range(2):
        for edge in (0, nb + 1):
            for r in range(3):
                x0[f, edge, 8 * r : 8 * r + 8] = zero
            f1[f, edge] = zero

    def fill(j):
        cols = pl.ds(pl.multiple_of(j * 128, 128), 128)
        for f in range(2):
            x0[f, j + 1, 0:4] = zero[0:4]
            x0[f, j + 1, pl.ds(4, 8, stride=2)] = fbuf[f, 0:8, cols]
            x0[f, j + 1, pl.ds(5, 8, stride=2)] = pick(fbuf[f, 8:16, cols], 7 - sub)

    def edge_step(j):
        cols = pl.ds(pl.multiple_of(j * 128, 128), 128)
        jj = j + 1
        mids, nears, fars, forces, rims = [], [], [], [], []
        for f in range(2):
            mid = x0[f, jj, 4:12]
            up1, up2 = x0[f, jj, 2:10], x0[f, jj, 0:8]
            near, far = sideways(mid, x0[f, jj - 1, 4:12], x0[f, jj + 1, 4:12], lane)
            nears.append(near + (up1 + x0[f, jj, 6:14]))
            fars.append(far + (up2 + x0[f, jj, 8:16]))
            forces.append(0.25 * both_ends(None, nbuf[0, f, :, cols], 0, sub))
            mids.append(mid)
            rims.append((DIFFUSE[f] * NEAR) * up1 + (DIFFUSE[f] * FAR) * mid)
        new = stepped(mids[0], mids[1], nears, fars, forces, 1.0, 0.05)
        wins, qs = [], []
        for f in range(2):
            half = turn(new[f], 4)
            f1[f, jj] = new[f]
            win = jnp.where(sub < 4, rims[f], half)
            own[f, j] = win
            q = 0.25 * both_ends(None, nbuf[1, f, :, cols], 0, sub)
            q = q + (DIFFUSE[f] * FAR) * half
            q = q + jnp.where(sub >= 2, (DIFFUSE[f] * NEAR) * turn(new[f], 6), 0.0)
            own_q[f, j] = turn(q, 4)
            wins.append(win)
            qs.append(q)
        return wins, qs

    def pair(i):
        wins0, qs0 = edge_step(2 * i)
        wins1, qs1 = edge_step(2 * i + 1)
        for out, side in ((m_odd, parity), (m_even, 1 - parity)):
            at = 6 - 2 * (sub & 3) + side
            out[2 * i] = jnp.where(sub < 4, pick(wins0[0], at), pick(wins0[1], at))
            out[2 * i + 1] = jnp.where(sub < 4, pick(wins1[0], at), pick(wins1[1], at))
            at = 2 - 2 * (sub & 1) + side
            first = jnp.where((sub & 2) == 0, pick(qs0[0], at), pick(qs0[1], at))
            second = jnp.where((sub & 2) == 0, pick(qs1[0], at), pick(qs1[1], at))
            out[nb + i] = jnp.where(sub < 4, first, second)

    def loop(lo, hi, body, unroll):
        if hi > lo:
            lax.fori_loop(lo, hi, lambda i, c: (body(i), c)[1], 0, unroll=unroll)

    done = 0
    for c in range(chunks):
        copies[c][0].wait()
        loop(c * width, (c + 1) * width, fill, 4)
        copies[c][1].wait()
        ready = nb if c == chunks - 1 else (c + 1) * width - 2
        loop(done // 2, ready // 2, pair, 2)
        done = ready


def averaging(k, value, transpose):
    row = lax.broadcasted_iota(jnp.int32, (128, 128), 0)
    col = lax.broadcasted_iota(jnp.int32, (128, 128), 1)
    fine, coarse = (col, row) if transpose else (row, col)
    return jnp.where(coarse == 32 * k + (fine >> 2), jnp.float32(value), jnp.float32(0.0))


def lanes_averaged(held):
    groups = held.shape[1]
    total = jnp.zeros((groups * 8, 128), jnp.float32)
    for k in range(4):
        total = total + jnp.dot(
            held[k].reshape(groups * 8, 128),
            averaging(k, 1.0 / 16.0, False),
            preferred_element_type=jnp.float32,
            precision=lax.Precision.HIGHEST,
        )
    return total.reshape(groups, 8, 128)


def coarse_start_kernel(row_axis, x0, start, m_odd, m_even, held):
    nb = x0.shape[1] - 2
    groups = nb // 4
    sub = iota(0)
    parity = lax.rem(lax.axis_index(row_axis), 2)

    def group(g, carry):
        for k in range(4):
            sums = []
            for f in range(2):
                parts = []
                for r in (4, 12):
                    x = x0[f, 4 * g + k + 1, r : r + 8]
                    x = x + turn(x, 4)
                    parts.append(x + turn(x, 2))
                sums.append(jnp.where((sub & 3) < 2, parts[0], parts[1]))
            held[k, g] = jnp.where(sub < 4, sums[0], sums[1])
        return carry

    lax.fori_loop(0, groups, group, 0)
    zero = jnp.zeros((8, 128), jnp.float32)
    start[0] = zero
    start[groups + 1] = zero
    start[1 : groups + 1] = lanes_averaged(held)

    def message(i, carry):
        rims = []
        for h in range(2):
            c = start[2 * i + h + 1]
            rims.append(jnp.where((sub & 2) == 0, NEAR * c, 0.0) + FAR * pick(c, sub ^ 2))
        for out, side in ((m_odd, parity), (m_even, 1 - parity)):
            at = 4 * ((sub >> 1) & 1) + 2 * (sub & 1) + side
            out[i] = jnp.where(sub < 4, pick(rims[0], at), pick(rims[1], at))
        return carry

    lax.fori_loop(0, groups // 2, message, 0)


def inner_kernel(x0, f1, noise, p2, p3, n2, g1, g2):
    nb = x0.shape[1] - 2
    sub, lane = iota(0), iota(1)
    zero = jnp.zeros((8, 128), jnp.float32)
    for f in range(2):
        for edge in (0, nb + 1):
            g1[f, edge] = zero
            g2[f, edge] = zero
    half = sub >> 1
    down1 = jnp.where(sub < 6, sub + 2, 13 - sub)
    down2 = jnp.where(sub < 4, sub + 4, 11 - sub)

    def first(j, carry):
        cols = pl.ds(pl.multiple_of(j * 128, 128), 128)
        jj = j + 1
        mids, nears, fars, forces = [], [], [], []
        for f in range(2):
            mid = x0[f, jj, 12:20]
            near, far = sideways(mid, x0[f, jj - 1, 12:20], x0[f, jj + 1, 12:20], lane)
            nears.append(near + (x0[f, jj, 10:18] + pick(mid, down1)))
            fars.append(far + (x0[f, jj, 8:16] + pick(mid, down2)))
            forces.append(0.25 * both_ends(None, noise[0, f, :, cols], 4, sub))
            mids.append(mid)
        new = stepped(mids[0], mids[1], nears, fars, forces, 1.0, 0.05)
        for f in range(2):
            g1[f, jj] = new[f]
        return carry

    def second(j, carry):
        cols = pl.ds(pl.multiple_of(j * 128, 128), 128)
        jj = j + 1
        mids, nears, fars, forces = [], [], [], []
        tops, top_nears, top_fars, top_forces = [], [], [], []
        for f in range(2):
            mid, top = g1[f, jj], f1[f, jj]
            near, far = sideways(mid, g1[f, jj - 1], g1[f, jj + 1], lane)
            up1 = jnp.where(sub < 2, turn(top, 2), turn(mid, 2))
            up2 = jnp.where(sub < 4, turn(top, 4), turn(mid, 4))
            nears.append(near + (up1 + pick(mid, down1)))
            fars.append(far + (up2 + pick(mid, down2)))
            forces.append(0.25 * both_ends(None, noise[1, f, :, cols], 4, sub))
            mids.append(mid)
            near, far = sideways(top, f1[f, jj - 1], f1[f, jj + 1], lane)
            up1 = jnp.where(sub < 6, 0.0, turn(top, 2))
            low1 = jnp.where(sub < 6, turn(top, 6), turn(mid, 6))
            low2 = jnp.where(sub < 4, turn(top, 4), turn(mid, 4))
            top_nears.append(near + (up1 + low1))
            top_fars.append(far + low2)
            top_forces.append(0.25 * both_ends(None, noise[1, f, :, cols], 0, sub))
            tops.append(top)
        new = stepped(mids[0], mids[1], nears, fars, forces, 1.0, 0.05)
        part = stepped(tops[0], tops[1], top_nears, top_fars, top_forces, 1.0, 0.05)
        for f in range(2):
            g2[f, jj] = new[f]
            p2[f, j] = jnp.where(sub < 4, turn(part[f], 4), turn(new[f], 4))
        return carry

    def third(j, carry):
        cols = pl.ds(pl.multiple_of(j * 128, 128), 128)
        jj = j + 1
        mids, nears, fars, forces = [], [], [], []
        for f in range(2):
            mid = g2[f, jj]
            near, far = sideways(mid, g2[f, jj - 1], g2[f, jj + 1], lane)
            up1 = jnp.where(sub < 2, 0.0, turn(mid, 2))
            up2 = jnp.where(sub < 4, 0.0, turn(mid, 4))
            nears.append(near + (up1 + pick(mid, down1)))
            fars.append(far + (up2 + pick(mid, down2)))
            forces.append(0.25 * both_ends(None, noise[2, f, :, cols], 4, sub))
            n2[f, j] = 0.25 * both_ends(None, noise[2, f, :, cols], 0, sub)
            mids.append(mid)
        new = stepped(mids[0], mids[1], nears, fars, forces, 1.0, 0.05)
        for f in range(2):
            p3[f, j] = new[f]
        return carry

    lax.fori_loop(0, nb, first, 0, unroll=2)
    lax.fori_loop(0, nb, second, 0)
    lax.fori_loop(0, nb, third, 0, unroll=2)


def coarse_kernel(row_axis, start, noise, m_odd, m_even, coarse, spread, held, push):
    groups = start.shape[0] - 2
    sub, lane = iota(0), iota(1)
    parity = lax.rem(lax.axis_index(row_axis), 2)
    mine = (sub & 1) == parity

    def gather_noise(g, carry):
        for k in range(4):
            cols = pl.ds(pl.multiple_of((4 * g + k) * 128, 128), 128)
            sums = []
            for f in range(2):
                total = noise[0, f, :, cols].astype(jnp.float32)
                total = total + noise[1, f, :, cols].astype(jnp.float32)
                total = total + noise[2, f, :, cols].astype(jnp.float32)
                parts = []
                for r in (0, 8):
                    x = total[r : r + 8]
                    x = x + turn(x, 7)
                    parts.append(x + turn(x, 6))
                sums.append(
                    jnp.where(
                        (sub & 1) == 0,
                        pick(parts[0], (sub & 2) * 2),
                        pick(parts[1], 4 - (sub & 2) * 2),
                    )
                )
            held[k, g] = jnp.where(sub < 4, sums[0], sums[1])
        return carry

    lax.fori_loop(0, groups, gather_noise, 0)
    push[...] = lanes_averaged(held)

    is_a = sub < 4
    scale, react = 3.0 / 16.0, 0.15
    diffuse = jnp.where(is_a, DIFFUSE[0] * scale, DIFFUSE[1] * scale)
    order = jnp.where(sub < 1, 0, jnp.where(sub < 2, 2, jnp.where(sub < 3, 3, 1)))

    def update(g, carry):
        pairs = g // 2
        base = 4 * (g - 2 * pairs)
        c = start[g + 1]
        near, far = sideways(c, start[g], start[g + 2], lane)
        inward = jnp.where((sub & 2) == 0, sub + 2, sub ^ 1)
        near = near + pick(c, inward) + jnp.where((sub & 2) == 0, 0.0, turn(c, 2))
        far = far + pick(c, (sub & 4) + 3 - (sub & 3))
        at = base + (sub >> 1)
        rim = jnp.where(mine, pick(m_odd[pairs], at), pick(m_even[pairs], at))
        lap = NEAR * near + FAR * far + rim - 5.0 * c
        other = turn(c, 4)
        change = jnp.where(
            is_a, react * (c - c * c * c / 3.0 - other), (react * 0.08) * (other + 0.7 - 0.8 * c)
        )
        new = c + diffuse * lap + change + push[g]
        push[g] = new
        cols = pl.ds(pl.multiple_of(g * 128, 128), 128)
        for f in range(2):
            coarse[f, :, cols] = pick(new, order + 4 * f)[0:4]
        return carry

    lax.fori_loop(0, groups, update, 0)
    for k in range(4):
        held[k] = jnp.dot(
            push[...].reshape(groups * 8, 128),
            averaging(k, 1.0, True),
            preferred_element_type=jnp.float32,
            precision=lax.Precision.HIGHEST,
        ).reshape(groups, 8, 128)

    def spread_rows(g, carry):
        for k in range(4):
            x = held[k, g]
            for f in range(2):
                spread[4 * g + k, 2 * f] = pick(x, 4 * f + jnp.where(sub < 4, 0, 2))
                spread[4 * g + k, 2 * f + 1] = pick(x, 4 * f + jnp.where(sub < 4, 3, 1))
        return carry

    lax.fori_loop(0, groups, spread_rows, 0)


def post_kernel(
    row_axis, m_odd, m_even, own, own_q, p2, p3, n2, spread, fine, corr, g1, g2, fbuf, cbuf, sems
):
    nb = own.shape[1]
    chunks = 4
    width = nb // chunks
    sub, lane = iota(0), iota(1)
    place = lax.axis_index(row_axis)
    parity = lax.rem(place, 2)
    last = lax.axis_size(row_axis) - 1
    mine = (sub & 1) == parity
    outside = ((place == 0) & ((sub & 1) == 0)) | ((place == last) & ((sub & 1) == 1))
    keep = jnp.where(outside & (sub < 4), jnp.float32(0.0), jnp.float32(1.0))
    half = sub >> 1
    zero = jnp.zeros((8, 128), jnp.float32)
    for f in range(2):
        for edge in (0, nb + 1):
            for r in range(3):
                g1[f, edge, 8 * r : 8 * r + 8] = zero
            for r in range(2):
                g2[f, edge, 8 * r : 8 * r + 8] = zero
    close = [jnp.where(sub < 2, DIFFUSE[f] * NEAR, 0.0) for f in range(2)]
    wide = [jnp.where(sub < 4, DIFFUSE[f] * FAR, 0.0) for f in range(2)]
    even_rows = (2 * sub) & 7

    def first(j):
        odd, even = m_odd[j], m_even[j]
        for f in range(2):
            came = jnp.where(mine, pick(odd, half + 4 * f), pick(even, half + 4 * f))
            g1[f, j + 1, 0:8] = zero
            g1[f, j + 1, 8:16] = (came + own[f, j]) * keep
            g1[f, j + 1, 16:24] = zero

    def second_at(j, odd, even, base):
        jj = j + 1
        mids, nears, fars, forces, twos = [], [], [], [], []
        for f in range(2):
            mid = g1[f, jj, 8:16]
            low2 = g1[f, jj, 12:20]
            near, far = sideways(mid, g1[f, jj - 1, 8:16], g1[f, jj + 1, 8:16], lane)
            nears.append(near + (g1[f, jj, 6:14] + g1[f, jj, 10:18]))
            fars.append(far + (g1[f, jj, 4:12] + low2))
            at = (half & 1) + (2 * f + base)
            came = jnp.where(mine, pick(odd, at), pick(even, at))
            forces.append(jnp.where(sub < 4, came, own_q[f, j]))
            mids.append(mid)
            more = (DIFFUSE[f] * NEAR) * g1[f, jj, 14:22] + (DIFFUSE[f] * FAR) * low2
            g2[f, jj, 8:16] = p2[f, j] + more
        new = stepped(mids[0], mids[1], nears, fars, forces, 1.0, 0.05)
        for f in range(2):
            g2[f, jj, 0:8] = new[f] * keep

    def second(i):
        odd, even = m_odd[nb + i], m_even[nb + i]
        second_at(2 * i, odd, even, 0)
        second_at(2 * i + 1, odd, even, 4)

    def third(j):
        cols = pl.ds(pl.multiple_of(j * 128, 128), 128)
        jj = j + 1
        mids, nears, fars, forces, lows = [], [], [], [], []
        for f in range(2):
            mid = g2[f, jj, 4:12]
            low2 = g2[f, jj, 8:16]
            near, far = sideways(mid, g2[f, jj - 1, 4:12], g2[f, jj + 1, 4:12], lane)
            nears.append(near + (g2[f, jj, 2:10] + g2[f, jj, 6:14]))
            fars.append(far + (g2[f, jj, 0:8] + low2))
            forces.append(n2[f, j])
            mids.append(mid)
            lows.append(p3[f, j] + close[f] * turn(low2, 6) + wide[f] * low2)
        new = stepped(mids[0], mids[1], nears, fars, forces, 1.0, 0.05)
        for f in range(2):
            top = jnp.where(sub < 4, pick(new[f], even_rows), pick(lows[f], even_rows))
            low = jnp.where(sub < 4, pick(lows[f], 7 - even_rows), pick(new[f], 7 - even_rows))
            fbuf[f, 0:8, cols] = top
            fbuf[f, 8:16, cols] = low
            cbuf[f, 0:8, cols] = top - spread[j, 2 * f]
            cbuf[f, 8:16, cols] = low - spread[j, 2 * f + 1]

    def loop(lo, hi, body, unroll):
        if hi > lo:
            lax.fori_loop(lo, hi, lambda i, c: (body(i), c)[1], 0, unroll=unroll)

    copies = []
    at1 = at2 = at3 = 0
    for c in range(chunks):
        end = (c + 1) * width
        end1, end2 = min(nb, end + 4), min(nb, end + 2)
        loop(at1, end1, first, 4)
        loop(at2 // 2, end2 // 2, second, 1)
        loop(at3, end, third, 2)
        at1, at2, at3 = end1, end2, end
        cols = pl.ds(c * width * 128, width * 128)
        for n, (src, dst) in enumerate(((fbuf, fine), (cbuf, corr))):
            copies.append(
                pltpu.make_async_copy(src.at[:, :, cols], dst.at[:, :, cols], sems.at[n, c])
            )
            copies[-1].start()
    for copy in copies:
        copy.wait()


def in_vmem(x):
    return pltpu.with_memory_space_constraint(x, pltpu.VMEM)


def spec(space=pltpu.VMEM):
    return pl.BlockSpec(memory_space=space)


def params(mib):
    return pltpu.CompilerParams(vmem_limit_bytes=mib * MIB)


def shards(count, fine_state, noise):
    f32, bf16 = jnp.float32, jnp.bfloat16
    wide = fine_state.shape[2]
    nb = wide // 128
    groups = nb // 4
    vmem = pltpu.VMEM

    pairs = [(i, i + 1) for i in range(1, count - 1, 2)]
    odd = pairs + [(b, a) for a, b in pairs]
    pairs = [(i, i + 1) for i in range(0, count - 1, 2)]
    even = pairs + [(b, a) for a, b in pairs]

    m_odd, m_even, x0, f1, own, own_q = pl.pallas_call(
        functools.partial(pre_kernel, "row"),
        out_shape=(
            vmem((nb + nb // 2, 8, 128), f32),
            vmem((nb + nb // 2, 8, 128), f32),
            vmem((2, nb + 2, 24, 128), f32),
            vmem((2, nb + 2, 8, 128), f32),
            vmem((2, nb, 8, 128), f32),
            vmem((2, nb, 8, 128), f32),
        ),
        in_specs=[spec(pl.ANY), spec(pl.ANY)],
        out_specs=[spec()] * 6,
        scratch_shapes=[
            vmem((2, 16, wide), f32),
            vmem((2, 2, 16, wide), bf16),
            pltpu.SemaphoreType.DMA((2, 4)),
        ],
        compiler_params=params(20),
        name="pre",
    )(fine_state, noise)
    m_odd = lax.ppermute(m_odd, "row", odd)
    m_even = lax.ppermute(m_even, "row", even)

    start, c_odd, c_even = pl.pallas_call(
        functools.partial(coarse_start_kernel, "row"),
        out_shape=(
            vmem((groups + 2, 8, 128), f32),
            vmem((groups // 2, 8, 128), f32),
            vmem((groups // 2, 8, 128), f32),
        ),
        in_specs=[spec()],
        out_specs=[spec()] * 3,
        scratch_shapes=[vmem((4, groups, 8, 128), f32)],
        compiler_params=params(20),
        name="coarse_start",
    )(in_vmem(x0))
    c_odd = lax.ppermute(c_odd, "row", odd)
    c_even = lax.ppermute(c_even, "row", even)

    p2, p3, n2 = pl.pallas_call(
        inner_kernel,
        out_shape=(
            vmem((2, nb, 8, 128), f32),
            vmem((2, nb, 8, 128), f32),
            vmem((2, nb, 8, 128), f32),
        ),
        in_specs=[spec()] * 3,
        out_specs=[spec()] * 3,
        scratch_shapes=[vmem((2, nb + 2, 8, 128), f32)] * 2,
        compiler_params=params(20),
        name="inner",
    )(in_vmem(x0), in_vmem(f1), noise)

    coarse, spread = pl.pallas_call(
        functools.partial(coarse_kernel, "row"),
        out_shape=(
            jax.ShapeDtypeStruct((2, 4, groups * 128), f32),
            vmem((nb, 4, 8, 128), f32),
        ),
        in_specs=[spec()] * 4,
        out_specs=[spec()] * 2,
        scratch_shapes=[vmem((4, groups, 8, 128), f32), vmem((groups, 8, 128), f32)],
        compiler_params=params(20),
        name="coarse",
    )(in_vmem(start), noise, in_vmem(c_odd), in_vmem(c_even))

    fine, corr = pl.pallas_call(
        functools.partial(post_kernel, "row"),
        out_shape=(
            jax.ShapeDtypeStruct((2, 16, wide), f32),
            jax.ShapeDtypeStruct((2, 16, wide), f32),
        ),
        in_specs=[spec()] * 8,
        out_specs=[spec(pl.ANY)] * 2,
        scratch_shapes=[
            vmem((2, nb + 2, 24, 128), f32),
            vmem((2, nb + 2, 16, 128), f32),
            vmem((2, 16, wide), f32),
            vmem((2, 16, wide), f32),
            pltpu.SemaphoreType.DMA((2, 4)),
        ],
        compiler_params=params(24),
        name="post",
    )(*(in_vmem(x) for x in (m_odd, m_even, own, own_q, p2, p3, n2, spread)))
    return fine, coarse, corr


def solution(mesh):
    rows = P("sample", "row", None)
    return jax.shard_map(
        functools.partial(shards, mesh.shape["row"]),
        mesh=mesh,
        in_specs=(rows, P("sample", None, "row", None)),
        out_specs=(rows, rows, rows),
        check_vma=False,
    )
```

profile of v0, /device:TPU:6, one launch (start us, length us, event | category | flops | bytes accessed | tf_op | source)
XLA Modules:
  0.0 64.4 jit_solution(5121343423192181450)
XLA Ops:
  0.6 0.0 copy-start
  0.6 1.9 %copy-done = bf16[3,2,16,16384]{3,2,1,0:T(8,128)(2,1)S(1)} copy-done((bf16[3,2,16,16384]{3,2,1,0:T(8,128)(2,1)S(1)}, bf16[3,2,16,16384]{3,2,1,0:T(8,128)(2,1)}, u32[]{:S(2)}) %copy-start) | copy-done | bytes 3145752
  2.5 0.0 copy-start.2
  2.5 1.6 %copy-done.2 = f32[2,16,16384]{2,1,0:T(8,128)S(1)} copy-done((f32[2,16,16384]{2,1,0:T(8,128)S(1)}, f32[2,16,16384]{2,1,0:T(8,128)}, u32[]{:S(2)}) %copy-start.2) | copy-done | bytes 2097176
  4.1 4.5 %pre.1 = (f32[192,8,128]{2,1,0:T(8,128)S(1)}, f32[192,8,128]{2,1,0:T(8,128)S(1)}, f32[2,130,24,128]{3,2,1,0:T(8,128)S(1)}, f32[2,130,8,128]{3,2,1,0:T(8,128)S(1)...) custom-call(f32[2,16,16384]{2,1,0:T(8,128)S(1)} %copy-done.2, bf16[3,2,16,16384]{3,2,1,0:T(8,128)(2,1)S(1)} %copy-done), custom_call_target="tpu_custom_call" | custom-call | tf_op jit(solution)/shard_map/pre/pallas_call | solution.py:486
  8.6 0.0 copy-start.1
  8.6 6.8 %collective-permute-start = (f32[192,8,128]{2,1,0:T(8,128)S(1)}, f32[192,8,128]{2,1,0:T(8,128)S(1)}, u32[]{:S(2)}, u32[]{:S(2)}) collective-permute-start(f32[192,8,128]{2,1,0:T(8,128)S(1)} %get-tuple-element.19), channel_id=1, source_target_pairs={{1,2},{3,4},{5,6},{7,8},{9,10},{11,12},{13,14},{15,16},{17,18},{19... | collective-permute-start | bytes 2359304 | tf_op jit(solution)/shard_map/ppermute | solution.py:506
  15.4 0.1 collective-permute-start.1
  15.5 1.3 %coarse_start.1 = (f32[34,8,128]{2,1,0:T(8,128)S(1)}, f32[16,8,128]{2,1,0:T(8,128)S(1)}, f32[16,8,128]{2,1,0:T(8,128)S(1)}) custom-call(f32[2,130,24,128]{3,2,1,0:T(8,128)S(1)} %get-tuple-element.23.x0), custom_call_target="tpu_custom_call" | custom-call | tf_op jit(solution)/shard_map/coarse_start/pallas_call | solution.py:509
  16.8 3.1 %collective-permute-start.2 = (f32[16,8,128]{2,1,0:T(8,128)S(1)}, f32[16,8,128]{2,1,0:T(8,128)S(1)}, u32[]{:S(2)}, u32[]{:S(2)}) collective-permute-start(f32[16,8,128]{2,1,0:T(8,128)S(1)} %get-tuple-element.29), channel_id=1, source_target_pairs={{1,2},{3,4},{5,6},{7,8},{9,10},{11,12},{13,14},{15,16},{17,18},{19... | collective-permute-start | bytes 196616 | tf_op jit(solution)/shard_map/ppermute | solution.py:522
  19.9 0.9 %collective-permute-start.3 = (f32[16,8,128]{2,1,0:T(8,128)S(1)}, f32[16,8,128]{2,1,0:T(8,128)S(1)}, u32[]{:S(2)}, u32[]{:S(2)}) collective-permute-start(f32[16,8,128]{2,1,0:T(8,128)S(1)} %get-tuple-element.30), channel_id=1, source_target_pairs={{0,1},{2,3},{4,5},{6,7},{8,9},{10,11},{12,13},{14,15},{16,17},{18,... | collective-permute-start | bytes 196616 | tf_op jit(solution)/shard_map/ppermute | solution.py:523
  20.8 0.0 copy-done.1
  20.8 23.4 %inner.1 = (f32[2,128,8,128]{3,2,1,0:T(8,128)S(1)}, f32[2,128,8,128]{3,2,1,0:T(8,128)S(1)}, f32[2,128,8,128]{3,2,1,0:T(8,128)S(1)}) custom-call(f32[2,130,24,128]{3,2,1,0:T(8,128)S(1)} %get-tuple-element.23.x0, f32[2,130,8,128]{3,2,1,0:T(8,128)S(1)} %get-tuple-element.24.f1, bf16[3,2,16,16384]{3,2,1,0:T(8,128)(2,1)S(1)} %copy-done.1), custom_call_target="tpu_custom_call" | custom-call | tf_op jit(solution)/shard_map/inner/pallas_call | solution.py:525
  44.3 0.0 collective-permute-done.2.m_odd
  44.3 0.0 collective-permute-done.3.m_even
  44.3 6.7 %coarse.1 = (f32[2,4,4096]{2,1,0:T(4,128)}, f32[128,4,8,128]{3,2,1,0:T(8,128)S(1)}) custom-call(f32[34,8,128]{2,1,0:T(8,128)S(1)} %get-tuple-element.28.start, bf16[3,2,16,16384]{3,2,1,0:T(8,128)(2,1)S(1)} %copy-done.1, f32[16,8,128]{2,1,0:T(8,128)S(1)} %collective-permute-done.2.m_odd, f32[16,8,128]{2,1,0:T(8,128)S(1)} %collective-permute-done.3.m_even), custom_call_target="tpu_custom_call" | custom-call | tf_op jit(solution)/shard_map/coarse/pallas_call | solution.py:539
  51.0 0.0 collective-permute-done.m_odd
  51.0 0.0 collective-permute-done.1.m_even
  51.0 13.3 %post.1 = (f32[2,16,16384]{2,1,0:T(8,128)}, f32[2,16,16384]{2,1,0:T(8,128)}) custom-call(f32[192,8,128]{2,1,0:T(8,128)S(1)} %collective-permute-done.m_odd, f32[192,8,128]{2,1,0:T(8,128)S(1)} %collective-permute-done.1.m_even, f32[2,128,8,128]{3,2,1,0:T(8,128)S(1)} %get-tuple-element.21.own, f32[2,128,8,128]{3,2,1,0:T(8,128)S(1)} %get-tuple-element.22.own_q, ...), custom_call_target="tpu_custom_call" | custom-call | tf_op jit(solution)/shard_map/post/pallas_call | solution.py:552
Async XLA Ops:
  0.6 1.9 %copy-start = (bf16[3,2,16,16384]{3,2,1,0:T(8,128)(2,1)S(1)}, bf16[3,2,16,16384]{3,2,1,0:T(8,128)(2,1)}, u32[]{:S(2)}) copy-start(bf16[3,2,16,16384]{3,2,1,0:T(8,128)(2,1)} %noise.3) | copy-start | bytes 9437188
  2.5 1.6 %copy-start.2 = (f32[2,16,16384]{2,1,0:T(8,128)S(1)}, f32[2,16,16384]{2,1,0:T(8,128)}, u32[]{:S(2)}) copy-start(f32[2,16,16384]{2,1,0:T(8,128)} %f_hbm.1) | copy-start | bytes 6291460
  8.6 12.2 %copy-start.1 = (bf16[3,2,16,16384]{3,2,1,0:T(8,128)(2,1)S(1)}, bf16[3,2,16,16384]{3,2,1,0:T(8,128)(2,1)}, u32[]{:S(2)}) copy-start(bf16[3,2,16,16384]{3,2,1,0:T(8,128)(2,1)} %noise.3) | copy-start | bytes 9437188
  8.6 42.4 %collective-permute-start = (f32[192,8,128]{2,1,0:T(8,128)S(1)}, f32[192,8,128]{2,1,0:T(8,128)S(1)}, u32[]{:S(2)}, u32[]{:S(2)}) collective-permute-start(f32[192,8,128]{2,1,0:T(8,128)S(1)} %get-tuple-element.19), channel_id=1, source_target_pairs={{1,2},{3,4},{5,6},{7,8},{9,10},{11,12},{13,14},{15,16},{17,18},{19... | collective-permute-start | bytes 2359304 | tf_op jit(solution)/shard_map/ppermute | solution.py:506
  15.4 35.6 %collective-permute-start.1 = (f32[192,8,128]{2,1,0:T(8,128)S(1)}, f32[192,8,128]{2,1,0:T(8,128)S(1)}, u32[]{:S(2)}, u32[]{:S(2)}) collective-permute-start(f32[192,8,128]{2,1,0:T(8,128)S(1)} %get-tuple-element.20), channel_id=1, source_target_pairs={{0,1},{2,3},{4,5},{6,7},{8,9},{10,11},{12,13},{14,15},{16,17},{18,... | collective-permute-start | bytes 2359304 | tf_op jit(solution)/shard_map/ppermute | solution.py:507
  16.8 27.5 %collective-permute-start.2 = (f32[16,8,128]{2,1,0:T(8,128)S(1)}, f32[16,8,128]{2,1,0:T(8,128)S(1)}, u32[]{:S(2)}, u32[]{:S(2)}) collective-permute-start(f32[16,8,128]{2,1,0:T(8,128)S(1)} %get-tuple-element.29), channel_id=1, source_target_pairs={{1,2},{3,4},{5,6},{7,8},{9,10},{11,12},{13,14},{15,16},{17,18},{19... | collective-permute-start | bytes 196616 | tf_op jit(solution)/shard_map/ppermute | solution.py:522
  19.9 24.4 %collective-permute-start.3 = (f32[16,8,128]{2,1,0:T(8,128)S(1)}, f32[16,8,128]{2,1,0:T(8,128)S(1)}, u32[]{:S(2)}, u32[]{:S(2)}) collective-permute-start(f32[16,8,128]{2,1,0:T(8,128)S(1)} %get-tuple-element.30), channel_id=1, source_target_pairs={{0,1},{2,3},{4,5},{6,7},{8,9},{10,11},{12,13},{14,15},{16,17},{18,... | collective-permute-start | bytes 196616 | tf_op jit(solution)/shard_map/ppermute | solution.py:523
where the time goes:
time: 64.5 us; the launch traced here: 64.4 us
  Pallas kernels  49.3 us (76%)
  starting transfers between devices  10.9 us (17%)
  local copies, waits for them, and re-layouts  3.48 us (5%)
  between operations  0.71 us (1%)
    pallas_call x1, Pallas kernels, shards(): pl.pallas_call(inner_kernel, out_shape=(vmem((2, nb, 8, 128), f32), vmem(...  23.4 us
    pallas_call x1, Pallas kernels, shards(): pl.pallas_call(functools.partial(post_kernel, 'row'), out_shape=(jax.Shap...  13.3 us
    ppermute x1, starting transfers between devices, shards(): m_odd = lax.ppermute(m_odd, 'row', odd)  6.8 us
    pallas_call x1, Pallas kernels, shards(): pl.pallas_call(functools.partial(coarse_kernel, 'row'), out_shape=(jax.Sh...  6.74 us
    pallas_call x1, Pallas kernels, shards(): pl.pallas_call(functools.partial(pre_kernel, 'row'), out_shape=(vmem((nb...  4.5 us
    unnamed x6, local copies, waits for them, and re-layouts  3.48 us
    ppermute x1, starting transfers between devices, shards(): c_odd = lax.ppermute(c_odd, 'row', odd)  3.07 us
  transfers between devices with their start and end apart: 4, of which 0 were waited for; matrix products, arithmetic and copies ran while one was open for 0% of the time, Pallas kernels for 49%

commit v1 on v0

v1 whole, which is shorter than its diff:
```python
import functools

import jax
import jax.numpy as jnp
from jax import lax
from jax.experimental import pallas as pl
from jax.experimental.pallas import tpu as pltpu
from jax.sharding import PartitionSpec as P

NEAR, FAR = 4.0 / 3.0, -1.0 / 12.0
DIFFUSE = (0.15, 0.05)
MIB = 1 << 20
CHUNKS = 4


def iota(dim):
    return lax.broadcasted_iota(jnp.int32, (8, 128), dim)


def pick(x, index):
    return jnp.take_along_axis(x, index, axis=0, mode="promise_in_bounds")


def turn(x, steps):
    return pltpu.roll(x, steps, 0)


def sideways(mid, left, right, lane):
    near = pltpu.roll(jnp.where(lane == 127, left, mid), 1, 1) + pltpu.roll(
        jnp.where(lane == 0, right, mid), 127, 1
    )
    far = pltpu.roll(jnp.where(lane >= 126, left, mid), 2, 1) + pltpu.roll(
        jnp.where(lane < 2, right, mid), 126, 1
    )
    return near, far


def stepped(a, b, near, far, force, scale, react):
    da, db = DIFFUSE[0] * scale, DIFFUSE[1] * scale
    new_a = a * ((1.0 + react - 5.0 * da) - (react / 3.0) * (a * a)) - react * b
    new_a = new_a + (da * NEAR) * near[0] + (da * FAR) * far[0] + force[0]
    low = 0.08 * react
    new_b = b * (1.0 - 5.0 * db - 0.8 * low) + low * a + 0.7 * low
    new_b = new_b + (db * NEAR) * near[1] + (db * FAR) * far[1] + force[1]
    return new_a, new_b


def both_ends(block, first, sub):
    block = block.astype(jnp.float32)
    half = sub >> 1
    top = pick(block[0:8], half + first)
    low = pick(block[8:16], 7 - first - half)
    return jnp.where((sub & 1) == 0, top, low)


def loop(lo, hi, body, unroll):
    if hi > lo:
        lax.fori_loop(lo, hi, lambda i, c: (body(i), c)[1], 0, unroll=unroll)


def whole_part(length, most):
    return max((d for d in range(1, most + 1) if length % d == 0), default=1)


def block_columns(j):
    return pl.ds(pl.multiple_of(j * 128, 128), 128)


def selection(k, value, transpose):
    shape = (256, 128)
    row = lax.broadcasted_iota(jnp.int32, shape, 0) & 127
    col = lax.broadcasted_iota(jnp.int32, shape, 1)
    fine, coarse = (col, row) if transpose else (row, col)
    return jnp.where(coarse == 32 * k + (fine >> 2), value, 0.0).astype(jnp.bfloat16)


def in_two(x):
    high = x.astype(jnp.bfloat16)
    low = (x - high.astype(jnp.float32)).astype(jnp.bfloat16)
    return jnp.concatenate([high, low], axis=1)


def lanes_averaged(held):
    groups = held.shape[1]
    total = jnp.zeros((groups * 8, 128), jnp.float32)
    for k in range(4):
        total = total + jnp.dot(
            in_two(held[k].reshape(groups * 8, 128)),
            selection(k, 1.0 / 16.0, False),
            preferred_element_type=jnp.float32,
        )
    return total.reshape(groups, 8, 128)


def edge_rows(parity, split, x0, noise, m_odd, m_even, f1, own, own_q):
    sub, lane = iota(0), iota(1)
    strong = [jnp.where((sub & 6) == 2, DIFFUSE[f] * NEAR, 0.0) for f in range(2)]
    wins_at = [6 - 2 * (sub & 3) + side for side in (parity, 1 - parity)]
    qs_at = [2 - 2 * (sub & 1) + side for side in (parity, 1 - parity)]

    def step(j):
        cols = block_columns(j)
        jj = j + 1
        mids, nears, fars, forces, rims = [], [], [], [], []
        for f in range(2):
            mid, up1 = x0[f, jj, 8:16], x0[f, jj, 6:14]
            near, far = sideways(mid, x0[f, jj - 1, 8:16], x0[f, jj + 1, 8:16], lane)
            nears.append(near + (up1 + x0[f, jj, 10:18]))
            fars.append(far + (x0[f, jj, 4:12] + x0[f, jj, 12:20]))
            forces.append(0.25 * both_ends(noise[0, f, :, cols], 0, sub))
            mids.append(mid)
            rims.append((DIFFUSE[f] * NEAR) * up1 + (DIFFUSE[f] * FAR) * mid)
        new = stepped(mids[0], mids[1], nears, fars, forces, 1.0, 0.05)
        wins, qs = [], []
        for f in range(2):
            half = turn(new[f], 4)
            f1[f, jj] = new[f]
            win = jnp.where(sub < 4, rims[f], half)
            own[f, j] = win
            q = 0.25 * both_ends(noise[1, f, :, cols], 0, sub)
            q = q + (DIFFUSE[f] * FAR) * half + strong[f] * turn(new[f], 6)
            own_q[f, j] = turn(q, 4)
            wins.append(win)
            qs.append(q)
        return wins, qs

    def pair(i):
        wins0, qs0 = step(2 * i)
        wins1, qs1 = step(2 * i + 1)
        base = split[0]
        blocks = split[1] - split[0]
        for n, out in enumerate((m_odd, m_even)):
            at = wins_at[n]
            k = 2 * i - base
            out[k] = jnp.where(sub < 4, pick(wins0[0], at), pick(wins0[1], at))
            out[k + 1] = jnp.where(sub < 4, pick(wins1[0], at), pick(wins1[1], at))
            at = qs_at[n]
            first = jnp.where((sub & 2) == 0, pick(qs0[0], at), pick(qs0[1], at))
            second = jnp.where((sub & 2) == 0, pick(qs1[0], at), pick(qs1[1], at))
            out[blocks + i - base // 2] = jnp.where(sub < 4, first, second)

    loop(split[0] // 2, split[1] // 2, pair, 8)


def start_kernel(
    row_axis, split, f_hbm, n_hbm, m_odd, m_even, x0, f1, own, own_q, start, noise, fbuf, held, sems
):
    nb = x0.shape[1] - 2
    groups = nb // 4
    width = nb // CHUNKS
    first, rest = [], []
    for c in range(CHUNKS):
        cols = pl.ds(c * width * 128, width * 128)
        first.append(pltpu.make_async_copy(f_hbm.at[:, :, cols], fbuf.at[:, :, cols], sems.at[c]))
    sooner, later = pl.ds(0, split * 128), pl.ds(split * 128, (nb - split) * 128)
    early = pltpu.make_async_copy(
        n_hbm.at[0:2, :, :, sooner], noise.at[0:2, :, :, sooner], sems.at[CHUNKS]
    )
    rest.append(
        pltpu.make_async_copy(
            n_hbm.at[0:2, :, :, later], noise.at[0:2, :, :, later], sems.at[CHUNKS + 1]
        )
    )
    rest.append(pltpu.make_async_copy(n_hbm.at[2:3], noise.at[2:3], sems.at[CHUNKS + 2]))
    for copy in first + [early] + rest:
        copy.start()
    sub = iota(0)
    half = sub >> 1
    parity = lax.rem(lax.axis_index(row_axis), 2)
    zero = jnp.zeros((8, 128), jnp.float32)
    for f in range(2):
        for edge in (0, nb + 1):
            for r in range(3):
                x0[f, edge, 8 * r : 8 * r + 8] = zero
            f1[f, edge] = zero
    start[0] = zero
    start[groups + 1] = zero

    def block(j):
        cols = block_columns(j)
        sums = []
        for f in range(2):
            top, low = fbuf[f, 0:8, cols], fbuf[f, 8:16, cols]
            outer = jnp.where((sub & 1) == 0, pick(top, half), pick(low, 7 - half))
            inner = jnp.where((sub & 1) == 0, pick(top, half + 4), pick(low, 3 - half))
            x0[f, j + 1, 0:8] = zero
            x0[f, j + 1, 8:16] = outer
            x0[f, j + 1, 16:24] = inner
            parts = []
            for x in (outer, inner):
                x = x + turn(x, 4)
                parts.append(x + turn(x, 2))
            sums.append(jnp.where((sub & 3) < 2, parts[0], parts[1]))
        return jnp.where(sub < 4, sums[0], sums[1])

    def group(g):
        for k in range(4):
            held[k, g] = block(4 * g + k)

    for c in range(CHUNKS):
        first[c].wait()
        loop(c * width // 4, (c + 1) * width // 4, group, 4)
    start[1 : groups + 1] = lanes_averaged(held)
    offset = m_odd.shape[0] - groups // 2

    def message(i):
        rims = []
        for h in range(2):
            c = start[2 * i + h + 1]
            rims.append(jnp.where((sub & 2) == 0, NEAR * c, 0.0) + FAR * pick(c, sub ^ 2))
        for out, side in ((m_odd, parity), (m_even, 1 - parity)):
            at = (2 * sub + side) & 7
            out[offset + i] = jnp.where(sub < 4, pick(rims[0], at), pick(rims[1], at))

    loop(0, groups // 2, message, 8)
    early.wait()
    edge_rows(parity, (0, split), x0, noise, m_odd, m_even, f1, own, own_q)
    for copy in rest:
        copy.wait()


def edge_kernel(row_axis, split, x0, noise, f1_in, own_in, q_in, m_odd, m_even, f1, own, own_q):
    del f1_in, own_in, q_in
    parity = lax.rem(lax.axis_index(row_axis), 2)
    edge_rows(parity, (split, own.shape[1]), x0, noise, m_odd, m_even, f1, own, own_q)


def inner_kernel(x0, f1, noise, p2, p3, n2, g1, g2):
    nb = x0.shape[1] - 2
    sub, lane = iota(0), iota(1)
    zero = jnp.zeros((8, 128), jnp.float32)
    for f in range(2):
        for edge in (0, nb + 1):
            g1[f, edge] = zero
            g2[f, edge] = zero
    down1 = jnp.where(sub < 6, sub + 2, 13 - sub)
    down2 = jnp.where(sub < 4, sub + 4, 11 - sub)

    def first(j):
        cols = block_columns(j)
        jj = j + 1
        mids, nears, fars, forces = [], [], [], []
        for f in range(2):
            mid = x0[f, jj, 16:24]
            near, far = sideways(mid, x0[f, jj - 1, 16:24], x0[f, jj + 1, 16:24], lane)
            nears.append(near + (x0[f, jj, 14:22] + pick(mid, down1)))
            fars.append(far + (x0[f, jj, 12:20] + pick(mid, down2)))
            forces.append(0.25 * both_ends(noise[0, f, :, cols], 4, sub))
            mids.append(mid)
        new = stepped(mids[0], mids[1], nears, fars, forces, 1.0, 0.05)
        for f in range(2):
            g1[f, jj] = new[f]

    def second(j):
        cols = block_columns(j)
        jj = j + 1
        mids, nears, fars, forces = [], [], [], []
        tops, top_nears, top_fars, top_forces = [], [], [], []
        for f in range(2):
            mid, top = g1[f, jj], f1[f, jj]
            top2, mid2, top4, mid4 = turn(top, 2), turn(mid, 2), turn(top, 4), turn(mid, 4)
            low2 = jnp.where(sub < 4, top4, mid4)
            near, far = sideways(mid, g1[f, jj - 1], g1[f, jj + 1], lane)
            nears.append(near + (jnp.where(sub < 2, top2, mid2) + pick(mid, down1)))
            fars.append(far + (low2 + pick(mid, down2)))
            noises = noise[1, f, :, cols]
            forces.append(0.25 * both_ends(noises, 4, sub))
            mids.append(mid)
            near, far = sideways(top, f1[f, jj - 1], f1[f, jj + 1], lane)
            up1 = jnp.where(sub < 6, 0.0, top2)
            low1 = jnp.where(sub < 6, turn(top, 6), turn(mid, 6))
            top_nears.append(near + (up1 + low1))
            top_fars.append(far + low2)
            top_forces.append(0.25 * both_ends(noises, 0, sub))
            tops.append(top)
        new = stepped(mids[0], mids[1], nears, fars, forces, 1.0, 0.05)
        part = stepped(tops[0], tops[1], top_nears, top_fars, top_forces, 1.0, 0.05)
        for f in range(2):
            g2[f, jj] = new[f]
            p2[f, j] = jnp.where(sub < 4, turn(part[f], 4), turn(new[f], 4))

    def third(j):
        cols = block_columns(j)
        jj = j + 1
        mids, nears, fars, forces = [], [], [], []
        for f in range(2):
            mid = g2[f, jj]
            near, far = sideways(mid, g2[f, jj - 1], g2[f, jj + 1], lane)
            up1 = jnp.where(sub < 2, 0.0, turn(mid, 2))
            up2 = jnp.where(sub < 4, 0.0, turn(mid, 4))
            nears.append(near + (up1 + pick(mid, down1)))
            fars.append(far + (up2 + pick(mid, down2)))
            noises = noise[2, f, :, cols]
            forces.append(0.25 * both_ends(noises, 4, sub))
            n2[f, j] = 0.25 * both_ends(noises, 0, sub)
            mids.append(mid)
        new = stepped(mids[0], mids[1], nears, fars, forces, 1.0, 0.05)
        for f in range(2):
            p3[f, j] = new[f]

    loop(0, nb, first, 16)
    loop(0, nb, second, 8)
    loop(0, nb, third, 16)


def coarse_kernel(row_axis, start, noise, a_odd, a_even, coarse, spread, held, push):
    groups = start.shape[0] - 2
    offset = a_odd.shape[0] - groups // 2
    sub, lane = iota(0), iota(1)
    parity = lax.rem(lax.axis_index(row_axis), 2)
    mine = (sub & 1) == parity

    def gather_noise(g):
        for k in range(4):
            cols = block_columns(4 * g + k)
            sums = []
            for f in range(2):
                total = noise[0, f, :, cols].astype(jnp.float32)
                total = total + noise[1, f, :, cols].astype(jnp.float32)
                total = total + noise[2, f, :, cols].astype(jnp.float32)
                parts = []
                for r in (0, 8):
                    x = total[r : r + 8]
                    x = x + turn(x, 7)
                    parts.append(x + turn(x, 6))
                sums.append(
                    jnp.where(
                        (sub & 1) == 0,
                        pick(parts[0], (sub & 2) * 2),
                        pick(parts[1], 4 - (sub & 2) * 2),
                    )
                )
            held[k, g] = jnp.where(sub < 4, sums[0], sums[1])

    loop(0, groups, gather_noise, 2)
    push[...] = lanes_averaged(held)

    is_a = sub < 4
    scale, react = 3.0 / 16.0, 0.15
    diffuse = jnp.where(is_a, DIFFUSE[0] * scale, DIFFUSE[1] * scale)
    order = jnp.where(sub < 1, 0, jnp.where(sub < 2, 2, jnp.where(sub < 3, 3, 1)))
    inward = jnp.where((sub & 2) == 0, sub + 2, sub ^ 1)

    def update(i):
        odd, even = a_odd[offset + i], a_even[offset + i]
        for h in range(2):
            g = 2 * i + h
            c = start[g + 1]
            near, far = sideways(c, start[g], start[g + 2], lane)
            near = near + pick(c, inward) + jnp.where((sub & 2) == 0, 0.0, turn(c, 2))
            far = far + pick(c, (sub & 4) + 3 - (sub & 3))
            at = 4 * h + (sub >> 1)
            rim = jnp.where(mine, pick(odd, at), pick(even, at))
            lap = NEAR * near + FAR * far + rim - 5.0 * c
            other = turn(c, 4)
            change = jnp.where(
                is_a,
                react * (c - c * c * c / 3.0 - other),
                (react * 0.08) * (other + 0.7 - 0.8 * c),
            )
            new = c + diffuse * lap + change + push[g]
            push[g] = new
            cols = block_columns(g)
            for f in range(2):
                coarse[f, :, cols] = pick(new, order + 4 * f)[0:4]

    loop(0, groups // 2, update, 4)
    whole = in_two(push[...].reshape(groups * 8, 128))
    for k in range(4):
        held[k] = jnp.dot(
            whole, selection(k, 1.0, True), preferred_element_type=jnp.float32
        ).reshape(groups, 8, 128)

    def spread_rows(g):
        for k in range(4):
            x = held[k, g]
            for f in range(2):
                spread[4 * g + k, 2 * f] = pick(x, 4 * f + jnp.where(sub < 4, 0, 2))
                spread[4 * g + k, 2 * f + 1] = pick(x, 4 * f + jnp.where(sub < 4, 3, 1))

    loop(0, groups, spread_rows, 4)


def finish(
    row_axis, spans, base, m_odd, m_even, own, own_q, p2, p3, n2, spread, fine, corr, g1, g2, fbuf, cbuf, sems
):
    nb = own.shape[1]
    blocks = base[1] - base[0]
    sub, lane = iota(0), iota(1)
    place = lax.axis_index(row_axis)
    parity = lax.rem(place, 2)
    last = lax.axis_size(row_axis) - 1
    mine = (sub & 1) == parity
    outside = ((place == 0) & ((sub & 1) == 0)) | ((place == last) & ((sub & 1) == 1))
    keep = jnp.where(outside & (sub < 4), jnp.float32(0.0), jnp.float32(1.0))
    half = sub >> 1
    zero = jnp.zeros((8, 128), jnp.float32)
    close = [jnp.where(sub < 2, DIFFUSE[f] * NEAR, 0.0) for f in range(2)]
    wide = [jnp.where(sub < 4, DIFFUSE[f] * FAR, 0.0) for f in range(2)]
    even_rows = (2 * sub) & 7

    def first(i):
        qs_odd = m_odd[blocks + i - base[0] // 2]
        qs_even = m_even[blocks + i - base[0] // 2]
        for h in range(2):
            j = 2 * i + h
            odd, even = m_odd[j - base[0]], m_even[j - base[0]]
            for f in range(2):
                came = jnp.where(mine, pick(odd, half + 4 * f), pick(even, half + 4 * f))
                at = (half & 1) + (2 * f + 4 * h)
                force = jnp.where(mine, pick(qs_odd, at), pick(qs_even, at))
                g1[f, j + 1, 0:8] = zero
                g1[f, j + 1, 8:16] = (came + own[f, j]) * keep
                g1[f, j + 1, 16:24] = jnp.where(sub < 4, force, own_q[f, j])

    def second(j):
        jj = j + 1
        mids, nears, fars, forces = [], [], [], []
        for f in range(2):
            mid = g1[f, jj, 8:16]
            near, far = sideways(mid, g1[f, jj - 1, 8:16], g1[f, jj + 1, 8:16], lane)
            turned = turn(mid, 4)
            up = turn(mid, 2)
            nears.append(near + (g1[f, jj, 6:14] + jnp.where(sub < 6, turn(mid, 6), 0.0)))
            fars.append(far + turned)
            forces.append(g1[f, jj, 16:24])
            mids.append(mid)
            g2[f, jj, 8:16] = p2[f, j] + (close[f] * up + wide[f] * turned)
        new = stepped(mids[0], mids[1], nears, fars, forces, 1.0, 0.05)
        for f in range(2):
            g2[f, jj, 0:8] = new[f] * keep

    def third(j):
        cols = block_columns(j)
        jj = j + 1
        mids, nears, fars, forces, deep = [], [], [], [], []
        for f in range(2):
            mid = g2[f, jj, 4:12]
            low2 = g2[f, jj, 8:16]
            near, far = sideways(mid, g2[f, jj - 1, 4:12], g2[f, jj + 1, 4:12], lane)
            nears.append(near + (g2[f, jj, 2:10] + g2[f, jj, 6:14]))
            fars.append(far + (g2[f, jj, 0:8] + low2))
            forces.append(n2[f, j])
            mids.append(mid)
            deep.append(p3[f, j] + (close[f] * turn(low2, 6) + wide[f] * low2))
        new = stepped(mids[0], mids[1], nears, fars, forces, 1.0, 0.05)
        for f in range(2):
            top = jnp.where(sub < 4, pick(new[f], even_rows), pick(deep[f], even_rows))
            low = jnp.where(sub < 4, pick(deep[f], 7 - even_rows), pick(new[f], 7 - even_rows))
            fbuf[f, 0:8, cols] = top
            fbuf[f, 8:16, cols] = low
            cbuf[f, 0:8, cols] = top - spread[j, 2 * f]
            cbuf[f, 8:16, cols] = low - spread[j, 2 * f + 1]

    for f in range(2):
        for edge in (0, nb + 1):
            for r in range(3):
                g1[f, edge, 8 * r : 8 * r + 8] = zero
            for r in range(2):
                g2[f, edge, 8 * r : 8 * r + 8] = zero
    copies = []
    for c, (span1, span2, span3) in enumerate(spans):
        loop(span1[0] // 2, span1[1] // 2, first, whole_part((span1[1] - span1[0]) // 2, 8))
        loop(*span2, second, whole_part(span2[1] - span2[0], 22))
        loop(*span3, third, whole_part(span3[1] - span3[0], 22))
        cols = pl.ds(span3[0] * 128, (span3[1] - span3[0]) * 128)
        for n, (src, dst) in enumerate(((fbuf, fine), (cbuf, corr))):
            copies.append(
                pltpu.make_async_copy(src.at[:, :, cols], dst.at[:, :, cols], sems.at[n, c])
            )
            copies[-1].start()
    for copy in copies:
        copy.wait()


def early_kernel(row_axis, split, *refs):
    ins, outs, carried, scratch = refs[:8], refs[8:10], refs[10:12], refs[12:]
    g1, g2 = scratch[:2]
    mid = split // 2
    spans = [
        ((0, split), (0, split - 1), (0, mid)),
        ((split, split), (split - 1, split - 1), (mid, split - 2)),
    ]
    finish(row_axis, spans, (0, split), *ins, *outs, *scratch)
    for f in range(2):
        for k in range(2):
            for r in range(3):
                carried[0][f, k, 8 * r : 8 * r + 8] = g1[f, split - 1 + k, 8 * r : 8 * r + 8]
            for r in range(2):
                carried[1][f, k, 8 * r : 8 * r + 8] = g2[f, split - 2 + k, 8 * r : 8 * r + 8]


def late_kernel(row_axis, split, *refs):
    ins, carried, outs, scratch = refs[:8], refs[8:10], refs[12:14], refs[14:]
    g1, g2 = scratch[:2]
    nb = ins[2].shape[1]
    for f in range(2):
        for k in range(2):
            for r in range(3):
                g1[f, split - 1 + k, 8 * r : 8 * r + 8] = carried[0][f, k, 8 * r : 8 * r + 8]
            for r in range(2):
                g2[f, split - 2 + k, 8 * r : 8 * r + 8] = carried[1][f, k, 8 * r : 8 * r + 8]
    mid = split + (nb - split) // 2
    spans = [
        ((split, nb), (split - 1, nb), (split - 2, mid)),
        ((nb, nb), (nb, nb), (mid, nb)),
    ]
    finish(row_axis, spans, (split, nb), *ins, *outs, *scratch)


def in_vmem(x):
    return pltpu.with_memory_space_constraint(x, pltpu.VMEM)


def in_hbm(x):
    return pltpu.with_memory_space_constraint(x, pltpu.HBM)


def spec(space):
    return pl.BlockSpec(memory_space=space)


def call(kernel, name, mib, ins, outs, scratch, hbm_ins=(), hbm_outs=(), aliases=None):
    return pl.pallas_call(
        kernel,
        out_shape=tuple(hbm_outs) + tuple(outs),
        in_specs=[spec(pltpu.VMEM)] * len(ins) + [spec(pltpu.HBM)] * len(hbm_ins),
        out_specs=(spec(pltpu.HBM),) * len(hbm_outs) + (spec(pltpu.VMEM),) * len(outs),
        scratch_shapes=scratch,
        input_output_aliases=aliases or {},
        compiler_params=pltpu.CompilerParams(vmem_limit_bytes=mib * MIB),
        name=name,
    )(*(in_vmem(x) for x in ins), *(in_hbm(x) for x in hbm_ins))


def shards(count, fine_state, noise):
    f32 = jnp.float32
    wide = fine_state.shape[2]
    nb = wide // 128
    groups = nb // 4
    split = nb // 2

    def vmem(*shape):
        return pltpu.VMEM(shape, f32)

    pairs = [(i, i + 1) for i in range(1, count - 1, 2)]
    odd = pairs + [(b, a) for a, b in pairs]
    pairs = [(i, i + 1) for i in range(0, count - 1, 2)]
    even = pairs + [(b, a) for a, b in pairs]

    a_rows = split + split // 2 + groups // 2
    a_odd, a_even, x0, f1, own, own_q, start, held_noise = call(
        functools.partial(start_kernel, "row", split),
        "start",
        16,
        [],
        [
            vmem(a_rows, 8, 128),
            vmem(a_rows, 8, 128),
            vmem(2, nb + 2, 24, 128),
            vmem(2, nb + 2, 8, 128),
            vmem(2, nb, 8, 128),
            vmem(2, nb, 8, 128),
            vmem(groups + 2, 8, 128),
            pltpu.VMEM(noise.shape, noise.dtype),
        ],
        [vmem(2, 16, wide), vmem(4, groups, 8, 128), pltpu.SemaphoreType.DMA((CHUNKS + 3,))],
        hbm_ins=[fine_state, noise],
    )
    a_odd = lax.ppermute(a_odd, "row", odd)
    a_even = lax.ppermute(a_even, "row", even)

    b_rows = (nb - split) + (nb - split) // 2
    b_odd, b_even, f1, own, own_q = call(
        functools.partial(edge_kernel, "row", split),
        "edge",
        16,
        [x0, held_noise, f1, own, own_q],
        [
            vmem(b_rows, 8, 128),
            vmem(b_rows, 8, 128),
            vmem(2, nb + 2, 8, 128),
            vmem(2, nb, 8, 128),
            vmem(2, nb, 8, 128),
        ],
        [],
        aliases={2: 2, 3: 3, 4: 4},
    )
    b_odd = lax.ppermute(b_odd, "row", odd)
    b_even = lax.ppermute(b_even, "row", even)

    p2, p3, n2 = call(
        inner_kernel,
        "inner",
        16,
        [x0, f1, held_noise],
        [vmem(2, nb, 8, 128)] * 3,
        [vmem(2, nb + 2, 8, 128)] * 2,
    )
    coarse, spread = call(
        functools.partial(coarse_kernel, "row"),
        "coarse",
        16,
        [start, held_noise, a_odd, a_even],
        [jax.ShapeDtypeStruct((2, 4, groups * 128), f32), vmem(nb, 4, 8, 128)],
        [vmem(4, groups, 8, 128), vmem(groups, 8, 128)],
    )
    work = [
        vmem(2, nb + 2, 24, 128),
        vmem(2, nb + 2, 16, 128),
        vmem(2, 16, wide),
        vmem(2, 16, wide),
        pltpu.SemaphoreType.DMA((2, 2)),
    ]
    whole = [jax.ShapeDtypeStruct((2, 16, wide), f32)] * 2
    fine, corr, last1, last2 = call(
        functools.partial(early_kernel, "row", split),
        "early",
        16,
        [a_odd, a_even, own, own_q, p2, p3, n2, spread],
        [vmem(2, 2, 24, 128), vmem(2, 2, 16, 128)],
        work,
        hbm_outs=whole,
    )
    fine, corr = call(
        functools.partial(late_kernel, "row", split),
        "late",
        16,
        [b_odd, b_even, own, own_q, p2, p3, n2, spread, last1, last2],
        [],
        work,
        hbm_ins=[fine, corr],
        hbm_outs=whole,
        aliases={10: 0, 11: 1},
    )
    return fine, coarse, corr


def solution(mesh):
    rows = P("sample", "row", None)
    return jax.shard_map(
        functools.partial(shards, mesh.shape["row"]),
        mesh=mesh,
        in_specs=(rows, P("sample", None, "row", None)),
        out_specs=(rows, rows, rows),
        check_vma=False,
    )
```

time: 64.5 us -> 33.9 us (0.53)
  Pallas kernels: 49.3 us -> 19.4 us
  local copies, waits for them, and re-layouts: 3.48 us -> 0 us
  waiting for transfers between devices: 0.01 us -> 3 us
    pallas_call x5 -> x6, Pallas kernels: 49.3 us -> 19.4 us  [call(): pl.pallas_call(kernel, out_shape=tuple(hbm_outs) + tuple(outs), in_specs=...]
    unnamed x6 -> x0, local copies, waits for them, and re-layouts: 3.48 us -> none
    ppermute x4, waiting for transfers between devices: 0.01 us -> 3 us  [the longest x1 1.69 us: shards(): a_even = lax.ppermute(a_even, 'row', even)]
  transfers between devices with their start and end apart: 4 -> 4, of which waited for: 0 -> 2; matrix products, arithmetic and copies ran while one was open for 0% -> 0% of each run, Pallas kernels for 49% -> 40%
where the time goes in v1:
time: 33.9 us; the launch traced here: 33.7 us
  Pallas kernels  19.4 us (57%)
  starting transfers between devices  10.6 us (31%)
  waiting for transfers between devices  3 us (9%)
  between operations  0.7 us (2%)
    pallas_call x6, Pallas kernels, call(): pl.pallas_call(kernel, out_shape=tuple(hbm_outs) + tuple(outs), in_specs=...  19.4 us
    ppermute x1, starting transfers between devices, shards(): a_odd = lax.ppermute(a_odd, 'row', odd)  6.54 us
    ppermute x1, starting transfers between devices, shards(): b_odd = lax.ppermute(b_odd, 'row', odd)  3.08 us
    ppermute x1, waiting for transfers between devices, shards(): a_even = lax.ppermute(a_even, 'row', even)  1.69 us
    ppermute x1, waiting for transfers between devices, shards(): b_even = lax.ppermute(b_even, 'row', even)  1.31 us
    ppermute x1, starting transfers between devices, shards(): b_even = lax.ppermute(b_even, 'row', even)  0.93 us
  transfers between devices with their start and end apart: 4, of which 2 were waited for; matrix products, arithmetic and copies ran while one was open for 0% of the time, Pallas kernels for 40%

profile of v1, /device:TPU:6, one launch (start us, length us, event | category | flops | bytes accessed | tf_op | source)
XLA Modules:
  0.0 33.7 jit_solution(11838821757056455142)
XLA Ops:
  0.6 3.0 %start.1 = (f32[112,8,128]{2,1,0:T(8,128)S(1)}, f32[112,8,128]{2,1,0:T(8,128)S(1)}, f32[2,130,24,128]{3,2,1,0:T(8,128)S(1)}, f32[2,130,8,128]{3,2,1,0:T(8,128)S(...) custom-call(f32[2,16,16384]{2,1,0:T(8,128)} %f_hbm.1, ...), custom_call_target="tpu_custom_call" | custom-call | tf_op jit(solution)/shard_map/start/pallas_call | solution.py:524
  3.7 6.5 %collective-permute-start.2 = (f32[112,8,128]{2,1,0:T(8,128)S(1)}, f32[112,8,128]{2,1,0:T(8,128)S(1)}, u32[]{:S(2)}, u32[]{:S(2)}) collective-permute-start(f32[112,8,128]{2,1,0:T(8,128)S(1)} %get-tuple-element.41), channel_id=1, source_target_pairs={{1,2},{3,4},{5,6},{7,8},{9,10},{11,12},{13,14},{15,16},{17,18},{19... | collective-permute-start | bytes 1376264 | tf_op jit(solution)/shard_map/ppermute | solution.py:570
  10.2 0.1 collective-permute-start.3
  10.3 1.0 %edge.1 = (f32[96,8,128]{2,1,0:T(8,128)S(1)}, f32[96,8,128]{2,1,0:T(8,128)S(1)}, f32[2,130,8,128]{3,2,1,0:T(8,128)S(1)}, f32[2,128,8,128]{3,2,1,0:T(8,128)S(1)}, f32[2,128,8,128]{3,2,1,0:T(8,128)S(1)}) custom-call(f32[2,130,24,128]{3,2,1,0:T(8,128)S(1)} %get-tuple-element.27.x0, ...), custom_call_target="tpu_custom_call", output_to_operand_aliasing={{2}: (2, {}), {3}: (3, {}), {4}: (4, {})} | custom-call | tf_op jit(solution)/shard_map/edge/pallas_call | solution.py:524
  11.3 3.1 %collective-permute-start = (f32[96,8,128]{2,1,0:T(8,128)S(1)}, f32[96,8,128]{2,1,0:T(8,128)S(1)}, u32[]{:S(2)}, u32[]{:S(2)}) collective-permute-start(f32[96,8,128]{2,1,0:T(8,128)S(1)} %get-tuple-element.32), channel_id=1, source_target_pairs={{1,2},{3,4},{5,6},{7,8},{9,10},{11,12},{13,14},{15,16},{17,18},{19... | collective-permute-start | bytes 1179656 | tf_op jit(solution)/shard_map/ppermute | solution.py:589
  14.4 0.9 %collective-permute-start.1 = (f32[96,8,128]{2,1,0:T(8,128)S(1)}, f32[96,8,128]{2,1,0:T(8,128)S(1)}, u32[]{:S(2)}, u32[]{:S(2)}) collective-permute-start(f32[96,8,128]{2,1,0:T(8,128)S(1)} %get-tuple-element.33), channel_id=1, source_target_pairs={{0,1},{2,3},{4,5},{6,7},{8,9},{10,11},{12,13},{14,15},{16,17},{18,... | collective-permute-start | bytes 1179656 | tf_op jit(solution)/shard_map/ppermute | solution.py:590
  15.3 6.7 %inner.1 = (f32[2,128,8,128]{3,2,1,0:T(8,128)S(1)}, f32[2,128,8,128]{3,2,1,0:T(8,128)S(1)}, f32[2,128,8,128]{3,2,1,0:T(8,128)S(1)}) custom-call(f32[2,130,24,128]{3,2,1,0:T(8,128)S(1)} %get-tuple-element.27.x0, f32[2,130,8,128]{3,2,1,0:T(8,128)S(1)} %get-tuple-element.36.f1, bf16[3,2,16,16384]{3,2,1,0:T(8,128)(2,1)S(1)} %get-tuple-element.28.noise), custom_call_target="tpu_custom_call" | custom-call | tf_op jit(solution)/shard_map/inner/pallas_call | solution.py:524
  22.0 0.0 collective-permute-done.2.a_odd.refs_0_
  22.1 1.7 %collective-permute-done.3.a_even.refs_1_ = f32[112,8,128]{2,1,0:T(8,128)S(1)} collective-permute-done((f32[112,8,128]{2,1,0:T(8,128)S(1)}, f32[112,8,128]{2,1,0:T(8,128)S(1)}, u32[]{:S(2)}, u32[]{:S(2)}) %collective-permute-start.3) | collective-permute-done | bytes 458784 | tf_op jit(solution)/shard_map/ppermute | solution.py:571
  23.7 2.9 %coarse.1 = (f32[2,4,4096]{2,1,0:T(4,128)}, f32[128,4,8,128]{3,2,1,0:T(8,128)S(1)}) custom-call(f32[34,8,128]{2,1,0:T(8,128)S(1)} %get-tuple-element.40.start, bf16[3,2,16,16384]{3,2,1,0:T(8,128)(2,1)S(1)} %get-tuple-element.28.noise, f32[112,8,128]{2,1,0:T(8,128)S(1)} %collective-permute-done.2.a_odd.refs_0_, ...), custom_call_target="tpu_custom_call" | custom-call | tf_op jit(solution)/shard_map/coarse/pallas_call | solution.py:524
  26.6 2.8 %early.1 = (f32[2,16,16384]{2,1,0:T(8,128)}, f32[2,16,16384]{2,1,0:T(8,128)}, f32[2,2,24,128]{3,2,1,0:T(8,128)S(1)}, f32[2,2,16,128]{3,2,1,0:T(8,128)S(1)}) custom-call(f32[112,8,128]{2,1,0:T(8,128)S(1)} %collective-permute-done.2.a_odd.refs_0_, f32[112,8,128]{2,1,0:T(8,128)S(1)} %collective-permute-done.3.a_even.refs_1_, ...), custom_call_target="tpu_custom_call" | custom-call | tf_op jit(solution)/shard_map/early/pallas_call | solution.py:524
  29.4 0.0 collective-permute-done.refs_0_
  29.4 1.3 %collective-permute-done.1.refs_1_ = f32[96,8,128]{2,1,0:T(8,128)S(1)} collective-permute-done((f32[96,8,128]{2,1,0:T(8,128)S(1)}, f32[96,8,128]{2,1,0:T(8,128)S(1)}, u32[]{:S(2)}, u32[]{:S(2)}) %collective-permute-start.1) | collective-permute-done | bytes 393248 | tf_op jit(solution)/shard_map/ppermute | solution.py:590
  30.7 3.0 %late.1 = (f32[2,16,16384]{2,1,0:T(8,128)}, f32[2,16,16384]{2,1,0:T(8,128)}) custom-call(f32[96,8,128]{2,1,0:T(8,128)S(1)} %collective-permute-done.refs_0_, f32[96,8,128]{2,1,0:T(8,128)S(1)} %collective-permute-done.1.refs_1_, f32[2,128,8,128]{3,2,1,0:T(8,128)S(1)} %get-tuple-element.34.refs_2_, ...), custom_call_target="tpu_custom_call", output_to_operand_aliasing={{0}: (10, {}), {1}: (11, {})} | custom-call | tf_op jit(solution)/shard_map/late/pallas_call | solution.py:524
Async XLA Ops:
  3.7 18.4 %collective-permute-start.2 = (f32[112,8,128]{2,1,0:T(8,128)S(1)}, f32[112,8,128]{2,1,0:T(8,128)S(1)}, u32[]{:S(2)}, u32[]{:S(2)}) collective-permute-start(f32[112,8,128]{2,1,0:T(8,128)S(1)} %get-tuple-element.41), channel_id=1, source_target_pairs={{1,2},{3,4},{5,6},{7,8},{9,10},{11,12},{13,14},{15,16},{17,18},{19... | collective-permute-start | bytes 1376264 | tf_op jit(solution)/shard_map/ppermute | solution.py:570
  10.2 13.5 %collective-permute-start.3 = (f32[112,8,128]{2,1,0:T(8,128)S(1)}, f32[112,8,128]{2,1,0:T(8,128)S(1)}, u32[]{:S(2)}, u32[]{:S(2)}) collective-permute-start(f32[112,8,128]{2,1,0:T(8,128)S(1)} %get-tuple-element.42), channel_id=1, source_target_pairs={{0,1},{2,3},{4,5},{6,7},{8,9},{10,11},{12,13},{14,15},{16,17},{18,... | collective-permute-start | bytes 1376264 | tf_op jit(solution)/shard_map/ppermute | solution.py:571
  11.3 18.1 %collective-permute-start = (f32[96,8,128]{2,1,0:T(8,128)S(1)}, f32[96,8,128]{2,1,0:T(8,128)S(1)}, u32[]{:S(2)}, u32[]{:S(2)}) collective-permute-start(f32[96,8,128]{2,1,0:T(8,128)S(1)} %get-tuple-element.32), channel_id=1, source_target_pairs={{1,2},{3,4},{5,6},{7,8},{9,10},{11,12},{13,14},{15,16},{17,18},{19... | collective-permute-start | bytes 1179656 | tf_op jit(solution)/shard_map/ppermute | solution.py:589
  14.4 16.3 %collective-permute-start.1 = (f32[96,8,128]{2,1,0:T(8,128)S(1)}, f32[96,8,128]{2,1,0:T(8,128)S(1)}, u32[]{:S(2)}, u32[]{:S(2)}) collective-permute-start(f32[96,8,128]{2,1,0:T(8,128)S(1)} %get-tuple-element.33), channel_id=1, source_target_pairs={{0,1},{2,3},{4,5},{6,7},{8,9},{10,11},{12,13},{14,15},{16,17},{18,... | collective-permute-start | bytes 1179656 | tf_op jit(solution)/shard_map/ppermute | solution.py:590

commit v2 on v1

--- a/solution.py
+++ b/solution.py
@@ -10,7 +10,8 @@
 NEAR, FAR = 4.0 / 3.0, -1.0 / 12.0
 DIFFUSE = (0.15, 0.05)
 MIB = 1 << 20
-CHUNKS = 4
+CHUNKS = 8
+MOST = 48
 
 
 def iota(dim):
@@ -58,8 +59,15 @@
         lax.fori_loop(lo, hi, lambda i, c: (body(i), c)[1], 0, unroll=unroll)
 
 
-def whole_part(length, most):
-    return max((d for d in range(1, most + 1) if length % d == 0), default=1)
+def long_loop(lo, hi, body, most):
+    if hi <= lo:
+        return
+    steps = -(-(hi - lo) // most)
+    each = (hi - lo) // steps
+    last = lo + (steps - 1) * each
+    loop(lo, last, body, each)
+    for j in range(last, hi):
+        body(j)
 
 
 def block_columns(j):
@@ -139,7 +147,7 @@
             second = jnp.where((sub & 2) == 0, pick(qs1[0], at), pick(qs1[1], at))
             out[blocks + i - base // 2] = jnp.where(sub < 4, first, second)
 
-    loop(split[0] // 2, split[1] // 2, pair, 8)
+    long_loop(split[0] // 2, split[1] // 2, pair, 18)
 
 
 def start_kernel(
@@ -225,7 +233,7 @@
     edge_rows(parity, (split, own.shape[1]), x0, noise, m_odd, m_even, f1, own, own_q)
 
 
-def inner_kernel(x0, f1, noise, p2, p3, n2, g1, g2):
+def inner_kernel(x0, f1, noise, start, p2, p3, n2, part, g1, g2, held):
     nb = x0.shape[1] - 2
     sub, lane = iota(0), iota(1)
     zero = jnp.zeros((8, 128), jnp.float32)
@@ -298,17 +306,15 @@
         for f in range(2):
             p3[f, j] = new[f]
 
-    loop(0, nb, first, 16)
-    loop(0, nb, second, 8)
-    loop(0, nb, third, 16)
-
-
-def coarse_kernel(row_axis, start, noise, a_odd, a_even, coarse, spread, held, push):
-    groups = start.shape[0] - 2
-    offset = a_odd.shape[0] - groups // 2
+    loop(0, nb, first, 32)
+    loop(0, nb, second, 32)
+    loop(0, nb, third, 32)
+    coarse_alone(start, noise, part, held)
+
+
+def coarse_alone(start, noise, part, held):
+    groups = part.shape[0]
     sub, lane = iota(0), iota(1)
-    parity = lax.rem(lax.axis_index(row_axis), 2)
-    mine = (sub & 1) == parity
 
     def gather_noise(g):
         for k in range(4):
@@ -332,40 +338,55 @@
                 )
             held[k, g] = jnp.where(sub < 4, sums[0], sums[1])
 
-    loop(0, groups, gather_noise, 2)
-    push[...] = lanes_averaged(held)
+    loop(0, groups, gather_noise, 4)
+    part[...] = lanes_averaged(held)
 
     is_a = sub < 4
     scale, react = 3.0 / 16.0, 0.15
     diffuse = jnp.where(is_a, DIFFUSE[0] * scale, DIFFUSE[1] * scale)
+    inward = jnp.where((sub & 2) == 0, sub + 2, sub ^ 1)
+
+    def update(g):
+        c = start[g + 1]
+        near, far = sideways(c, start[g], start[g + 2], lane)
+        near = near + pick(c, inward) + jnp.where((sub & 2) == 0, 0.0, turn(c, 2))
+        far = far + pick(c, (sub & 4) + 3 - (sub & 3))
+        lap = NEAR * near + FAR * far - 5.0 * c
+        other = turn(c, 4)
+        change = jnp.where(
+            is_a,
+            react * (c - c * c * c / 3.0 - other),
+            (react * 0.08) * (other + 0.7 - 0.8 * c),
+        )
+        part[g] = c + diffuse * lap + change + part[g]
+
+    loop(0, groups, update, 16)
+
+
+def coarse_kernel(row_axis, part, a_odd, a_even, coarse, spread, held, new):
+    groups = part.shape[0]
+    offset = a_odd.shape[0] - groups // 2
+    sub = iota(0)
+    parity = lax.rem(lax.axis_index(row_axis), 2)
+    mine = (sub & 1) == parity
+    scale = 3.0 / 16.0
+    diffuse = jnp.where(sub < 4, DIFFUSE[0] * scale, DIFFUSE[1] * scale)
     order = jnp.where(sub < 1, 0, jnp.where(sub < 2, 2, jnp.where(sub < 3, 3, 1)))
-    inward = jnp.where((sub & 2) == 0, sub + 2, sub ^ 1)
-
-    def update(i):
+
+    def add_rim(i):
         odd, even = a_odd[offset + i], a_even[offset + i]
         for h in range(2):
             g = 2 * i + h
-            c = start[g + 1]
-            near, far = sideways(c, start[g], start[g + 2], lane)
-            near = near + pick(c, inward) + jnp.where((sub & 2) == 0, 0.0, turn(c, 2))
-            far = far + pick(c, (sub & 4) + 3 - (sub & 3))
             at = 4 * h + (sub >> 1)
             rim = jnp.where(mine, pick(odd, at), pick(even, at))
-            lap = NEAR * near + FAR * far + rim - 5.0 * c
-            other = turn(c, 4)
-            change = jnp.where(
-                is_a,
-                react * (c - c * c * c / 3.0 - other),
-                (react * 0.08) * (other + 0.7 - 0.8 * c),
-            )
-            new = c + diffuse * lap + change + push[g]
-            push[g] = new
+            whole = part[g] + diffuse * rim
+            new[g] = whole
             cols = block_columns(g)
             for f in range(2):
-                coarse[f, :, cols] = pick(new, order + 4 * f)[0:4]
-
-    loop(0, groups // 2, update, 4)
-    whole = in_two(push[...].reshape(groups * 8, 128))
+                coarse[f, :, cols] = pick(whole, order + 4 * f)[0:4]
+
+    loop(0, groups // 2, add_rim, 8)
+    whole = in_two(new[...].reshape(groups * 8, 128))
     for k in range(4):
         held[k] = jnp.dot(
             whole, selection(k, 1.0, True), preferred_element_type=jnp.float32
@@ -378,7 +399,7 @@
                 spread[4 * g + k, 2 * f] = pick(x, 4 * f + jnp.where(sub < 4, 0, 2))
                 spread[4 * g + k, 2 * f + 1] = pick(x, 4 * f + jnp.where(sub < 4, 3, 1))
 
-    loop(0, groups, spread_rows, 4)
+    loop(0, groups, spread_rows, 8)
 
 
 def finish(
@@ -460,9 +481,9 @@
                 g2[f, edge, 8 * r : 8 * r + 8] = zero
     copies = []
     for c, (span1, span2, span3) in enumerate(spans):
-        loop(span1[0] // 2, span1[1] // 2, first, whole_part((span1[1] - span1[0]) // 2, 8))
-        loop(*span2, second, whole_part(span2[1] - span2[0], 22))
-        loop(*span3, third, whole_part(span3[1] - span3[0], 22))
+        long_loop(span1[0] // 2, span1[1] // 2, first, 16)
+        long_loop(*span2, second, MOST)
+        long_loop(*span3, third, MOST)
         cols = pl.ds(span3[0] * 128, (span3[1] - span3[0]) * 128)
         for n, (src, dst) in enumerate(((fbuf, fine), (cbuf, corr))):
             copies.append(
@@ -538,7 +559,7 @@
     wide = fine_state.shape[2]
     nb = wide // 128
     groups = nb // 4
-    split = nb // 2
+    split = nb // 2 + 8
 
     def vmem(*shape):
         return pltpu.VMEM(shape, f32)
@@ -589,19 +610,19 @@
     b_odd = lax.ppermute(b_odd, "row", odd)
     b_even = lax.ppermute(b_even, "row", even)
 
-    p2, p3, n2 = call(
+    p2, p3, n2, part = call(
         inner_kernel,
         "inner",
         16,
-        [x0, f1, held_noise],
-        [vmem(2, nb, 8, 128)] * 3,
-        [vmem(2, nb + 2, 8, 128)] * 2,
+        [x0, f1, held_noise, start],
+        [vmem(2, nb, 8, 128)] * 3 + [vmem(groups, 8, 128)],
+        [vmem(2, nb + 2, 8, 128)] * 2 + [vmem(4, groups, 8, 128)],
     )
     coarse, spread = call(
         functools.partial(coarse_kernel, "row"),
         "coarse",
         16,
-        [start, held_noise, a_odd, a_even],
+        [part, a_odd, a_even],
         [jax.ShapeDtypeStruct((2, 4, groups * 128), f32), vmem(nb, 4, 8, 128)],
         [vmem(4, groups, 8, 128), vmem(groups, 8, 128)],
     )

time: 33.9 us -> 33 us (0.973)
  Pallas kernels: 19.4 us -> 16.5 us
  waiting for transfers between devices: 3 us -> 5 us
    pallas_call x6, Pallas kernels: 19.4 us -> 16.5 us  [call(): pl.pallas_call(kernel, out_shape=tuple(hbm_outs) + tuple(outs), in_specs=...]
    ppermute x1, waiting for transfers between devices: 0.01 us -> 1.15 us  [shards(): a_odd = lax.ppermute(a_odd, 'row', odd)]
    ppermute x1, waiting for transfers between devices: 0.01 us -> 0.64 us  [shards(): b_odd = lax.ppermute(b_odd, 'row', odd)]
  transfers between devices with their start and end apart: 4 -> 4, of which waited for: 2 -> 4; matrix products, arithmetic and copies ran while one was open for 0% -> 0% of each run, Pallas kernels for 40% -> 35%
where the time goes in v2:
time: 33 us; the launch traced here: 32.9 us
  Pallas kernels  16.5 us (50%)
  starting transfers between devices  10.6 us (32%)
  waiting for transfers between devices  5 us (15%)
  between operations  0.68 us (2%)
    pallas_call x6, Pallas kernels, call(): pl.pallas_call(kernel, out_shape=tuple(hbm_outs) + tuple(outs), in_specs=...  16.5 us
    ppermute x1, starting transfers between devices, shards(): a_odd = lax.ppermute(a_odd, 'row', odd)  6.54 us
    ppermute x1, starting transfers between devices, shards(): b_odd = lax.ppermute(b_odd, 'row', odd)  3.08 us
    ppermute x1, waiting for transfers between devices, shards(): a_even = lax.ppermute(a_even, 'row', even)  1.76 us
    ppermute x1, waiting for transfers between devices, shards(): b_even = lax.ppermute(b_even, 'row', even)  1.45 us
    ppermute x1, waiting for transfers between devices, shards(): a_odd = lax.ppermute(a_odd, 'row', odd)  1.15 us
    ppermute x1, starting transfers between devices, shards(): b_even = lax.ppermute(b_even, 'row', even)  0.92 us
  transfers between devices with their start and end apart: 4, of which 4 were waited for; matrix products, arithmetic and copies ran while one was open for 0% of the time, Pallas kernels for 35%

profile of v2, /device:TPU:6, one launch (start us, length us, event | category | flops | bytes accessed | tf_op | source)
XLA Modules:
  0.0 32.9 jit_solution(1415145452087123050)
XLA Ops:
  0.6 3.0 %start.1 = (f32[124,8,128]{2,1,0:T(8,128)S(1)}, f32[124,8,128]{2,1,0:T(8,128)S(1)}, f32[2,130,24,128]{3,2,1,0:T(8,128)S(1)}, f32[2,130,8,128]{3,2,1,0:T(8,128)S(...) custom-call(f32[2,16,16384]{2,1,0:T(8,128)} %f_hbm.1, ...), custom_call_target="tpu_custom_call" | custom-call | tf_op jit(solution)/shard_map/start/pallas_call | solution.py:545
  3.6 6.5 %collective-permute-start.2 = (f32[124,8,128]{2,1,0:T(8,128)S(1)}, f32[124,8,128]{2,1,0:T(8,128)S(1)}, u32[]{:S(2)}, u32[]{:S(2)}) collective-permute-start(f32[124,8,128]{2,1,0:T(8,128)S(1)} %get-tuple-element.43), channel_id=1, source_target_pairs={{1,2},{3,4},{5,6},{7,8},{9,10},{11,12},{13,14},{15,16},{17,18},{19... | collective-permute-start | bytes 1523720 | tf_op jit(solution)/shard_map/ppermute | solution.py:591
  10.2 0.1 collective-permute-start.3
  10.3 0.8 %edge.1 = (f32[84,8,128]{2,1,0:T(8,128)S(1)}, f32[84,8,128]{2,1,0:T(8,128)S(1)}, f32[2,130,8,128]{3,2,1,0:T(8,128)S(1)}, f32[2,128,8,128]{3,2,1,0:T(8,128)S(1)}, f32[2,128,8,128]{3,2,1,0:T(8,128)S(1)}) custom-call(f32[2,130,24,128]{3,2,1,0:T(8,128)S(1)} %get-tuple-element.28.x0, ...), custom_call_target="tpu_custom_call", output_to_operand_aliasing={{2}: (2, {}), {3}: (3, {}), {4}: (4, {})} | custom-call | tf_op jit(solution)/shard_map/edge/pallas_call | solution.py:545
  11.1 3.1 %collective-permute-start = (f32[84,8,128]{2,1,0:T(8,128)S(1)}, f32[84,8,128]{2,1,0:T(8,128)S(1)}, u32[]{:S(2)}, u32[]{:S(2)}) collective-permute-start(f32[84,8,128]{2,1,0:T(8,128)S(1)} %get-tuple-element.33), channel_id=1, source_target_pairs={{1,2},{3,4},{5,6},{7,8},{9,10},{11,12},{13,14},{15,16},{17,18},{19... | collective-permute-start | bytes 1032200 | tf_op jit(solution)/shard_map/ppermute | solution.py:610
  14.2 0.9 %collective-permute-start.1 = (f32[84,8,128]{2,1,0:T(8,128)S(1)}, f32[84,8,128]{2,1,0:T(8,128)S(1)}, u32[]{:S(2)}, u32[]{:S(2)}) collective-permute-start(f32[84,8,128]{2,1,0:T(8,128)S(1)} %get-tuple-element.34), channel_id=1, source_target_pairs={{0,1},{2,3},{4,5},{6,7},{8,9},{10,11},{12,13},{14,15},{16,17},{18,... | collective-permute-start | bytes 1032200 | tf_op jit(solution)/shard_map/ppermute | solution.py:611
  15.1 6.8 %inner.1 = (f32[2,128,8,128]{3,2,1,0:T(8,128)S(1)}, f32[2,128,8,128]{3,2,1,0:T(8,128)S(1)}, f32[2,128,8,128]{3,2,1,0:T(8,128)S(1)}, f32[32,8,128]{2,1,0:T(8,128)S(1)}) custom-call(f32[2,130,24,128]{3,2,1,0:T(8,128)S(1)} %get-tuple-element.28.x0, f32[2,130,8,128]{3,2,1,0:T(8,128)S(1)} %get-tuple-element.37.f1, ...), custom_call_target="tpu_custom_call" | custom-call | tf_op jit(solution)/shard_map/inner/pallas_call | solution.py:545
  21.8 1.2 %collective-permute-done.2.a_odd.refs_0_ = f32[124,8,128]{2,1,0:T(8,128)S(1)} collective-permute-done((f32[124,8,128]{2,1,0:T(8,128)S(1)}, f32[124,8,128]{2,1,0:T(8,128)S(1)}, u32[]{:S(2)}, u32[]{:S(2)}) %collective-permute-start.2) | collective-permute-done | bytes 507936 | tf_op jit(solution)/shard_map/ppermute | solution.py:591
  23.0 1.8 %collective-permute-done.3.a_even.refs_1_ = f32[124,8,128]{2,1,0:T(8,128)S(1)} collective-permute-done((f32[124,8,128]{2,1,0:T(8,128)S(1)}, f32[124,8,128]{2,1,0:T(8,128)S(1)}, u32[]{:S(2)}, u32[]{:S(2)}) %collective-permute-start.3) | collective-permute-done | bytes 507936 | tf_op jit(solution)/shard_map/ppermute | solution.py:592
  24.8 1.2 %coarse.1 = (f32[2,4,4096]{2,1,0:T(4,128)}, f32[128,4,8,128]{3,2,1,0:T(8,128)S(1)}) custom-call(f32[32,8,128]{2,1,0:T(8,128)S(1)} %get-tuple-element.42.part, f32[124,8,128]{2,1,0:T(8,128)S(1)} %collective-permute-done.2.a_odd.refs_0_, f32[124,8,128]{2,1,0:T(8,128)S(1)} %collective-permute-done.3.a_even.refs_1_), custom_call_target="tpu_custom_call" | custom-call | tf_op jit(solution)/shard_map/coarse/pallas_call | solution.py:545
  25.9 2.7 %early.1 = (f32[2,16,16384]{2,1,0:T(8,128)}, f32[2,16,16384]{2,1,0:T(8,128)}, f32[2,2,24,128]{3,2,1,0:T(8,128)S(1)}, f32[2,2,16,128]{3,2,1,0:T(8,128)S(1)}) custom-call(f32[124,8,128]{2,1,0:T(8,128)S(1)} %collective-permute-done.2.a_odd.refs_0_, f32[124,8,128]{2,1,0:T(8,128)S(1)} %collective-permute-done.3.a_even.refs_1_, ...), custom_call_target="tpu_custom_call" | custom-call | tf_op jit(solution)/shard_map/early/pallas_call | solution.py:545
  28.6 0.6 %collective-permute-done.refs_0_ = f32[84,8,128]{2,1,0:T(8,128)S(1)} collective-permute-done((f32[84,8,128]{2,1,0:T(8,128)S(1)}, f32[84,8,128]{2,1,0:T(8,128)S(1)}, u32[]{:S(2)}, u32[]{:S(2)}) %collective-permute-start) | collective-permute-done | bytes 344096 | tf_op jit(solution)/shard_map/ppermute | solution.py:610
  29.2 1.4 %collective-permute-done.1.refs_1_ = f32[84,8,128]{2,1,0:T(8,128)S(1)} collective-permute-done((f32[84,8,128]{2,1,0:T(8,128)S(1)}, f32[84,8,128]{2,1,0:T(8,128)S(1)}, u32[]{:S(2)}, u32[]{:S(2)}) %collective-permute-start.1) | collective-permute-done | bytes 344096 | tf_op jit(solution)/shard_map/ppermute | solution.py:611
  30.7 2.2 %late.1 = (f32[2,16,16384]{2,1,0:T(8,128)}, f32[2,16,16384]{2,1,0:T(8,128)}) custom-call(f32[84,8,128]{2,1,0:T(8,128)S(1)} %collective-permute-done.refs_0_, f32[84,8,128]{2,1,0:T(8,128)S(1)} %collective-permute-done.1.refs_1_, f32[2,128,8,128]{3,2,1,0:T(8,128)S(1)} %get-tuple-element.35.refs_2_, ...), custom_call_target="tpu_custom_call", output_to_operand_aliasing={{0}: (10, {}), {1}: (11, {})} | custom-call | tf_op jit(solution)/shard_map/late/pallas_call | solution.py:545
Async XLA Ops:
  3.6 19.4 %collective-permute-start.2 = (f32[124,8,128]{2,1,0:T(8,128)S(1)}, f32[124,8,128]{2,1,0:T(8,128)S(1)}, u32[]{:S(2)}, u32[]{:S(2)}) collective-permute-start(f32[124,8,128]{2,1,0:T(8,128)S(1)} %get-tuple-element.43), channel_id=1, source_target_pairs={{1,2},{3,4},{5,6},{7,8},{9,10},{11,12},{13,14},{15,16},{17,18},{19... | collective-permute-start | bytes 1523720 | tf_op jit(solution)/shard_map/ppermute | solution.py:591
  10.2 14.6 %collective-permute-start.3 = (f32[124,8,128]{2,1,0:T(8,128)S(1)}, f32[124,8,128]{2,1,0:T(8,128)S(1)}, u32[]{:S(2)}, u32[]{:S(2)}) collective-permute-start(f32[124,8,128]{2,1,0:T(8,128)S(1)} %get-tuple-element.44), channel_id=1, source_target_pairs={{0,1},{2,3},{4,5},{6,7},{8,9},{10,11},{12,13},{14,15},{16,17},{18,... | collective-permute-start | bytes 1523720 | tf_op jit(solution)/shard_map/ppermute | solution.py:592
  11.1 18.2 %collective-permute-start = (f32[84,8,128]{2,1,0:T(8,128)S(1)}, f32[84,8,128]{2,1,0:T(8,128)S(1)}, u32[]{:S(2)}, u32[]{:S(2)}) collective-permute-start(f32[84,8,128]{2,1,0:T(8,128)S(1)} %get-tuple-element.33), channel_id=1, source_target_pairs={{1,2},{3,4},{5,6},{7,8},{9,10},{11,12},{13,14},{15,16},{17,18},{19... | collective-permute-start | bytes 1032200 | tf_op jit(solution)/shard_map/ppermute | solution.py:610
  14.2 16.5 %collective-permute-start.1 = (f32[84,8,128]{2,1,0:T(8,128)S(1)}, f32[84,8,128]{2,1,0:T(8,128)S(1)}, u32[]{:S(2)}, u32[]{:S(2)}) collective-permute-start(f32[84,8,128]{2,1,0:T(8,128)S(1)} %get-tuple-element.34), channel_id=1, source_target_pairs={{0,1},{2,3},{4,5},{6,7},{8,9},{10,11},{12,13},{14,15},{16,17},{18,... | collective-permute-start | bytes 1032200 | tf_op jit(solution)/shard_map/ppermute | solution.py:611

commit v3 on v2

--- a/solution.py
+++ b/solution.py
@@ -430,7 +430,6 @@
                 came = jnp.where(mine, pick(odd, half + 4 * f), pick(even, half + 4 * f))
                 at = (half & 1) + (2 * f + 4 * h)
                 force = jnp.where(mine, pick(qs_odd, at), pick(qs_even, at))
-                g1[f, j + 1, 0:8] = zero
                 g1[f, j + 1, 8:16] = (came + own[f, j]) * keep
                 g1[f, j + 1, 16:24] = jnp.where(sub < 4, force, own_q[f, j])
 
@@ -442,7 +441,8 @@
             near, far = sideways(mid, g1[f, jj - 1, 8:16], g1[f, jj + 1, 8:16], lane)
             turned = turn(mid, 4)
             up = turn(mid, 2)
-            nears.append(near + (g1[f, jj, 6:14] + jnp.where(sub < 6, turn(mid, 6), 0.0)))
+            up1 = jnp.where(sub < 2, 0.0, up)
+            nears.append(near + (up1 + jnp.where(sub < 6, turn(mid, 6), 0.0)))
             fars.append(far + turned)
             forces.append(g1[f, jj, 16:24])
             mids.append(mid)

time: 33 us -> 33 us (level)
  no operation moved by 1% of the time
where the time goes in v3:
time: 33 us; the launch traced here: 32.8 us
  Pallas kernels  16.5 us (50%)
  starting transfers between devices  10.6 us (32%)
  waiting for transfers between devices  4.99 us (15%)
  between operations  0.68 us (2%)
    pallas_call x6, Pallas kernels, call(): pl.pallas_call(kernel, out_shape=tuple(hbm_outs) + tuple(outs), in_specs=...  16.5 us
    ppermute x1, starting transfers between devices, shards(): a_odd = lax.ppermute(a_odd, 'row', odd)  6.54 us
    ppermute x1, starting transfers between devices, shards(): b_odd = lax.ppermute(b_odd, 'row', odd)  3.08 us
    ppermute x1, waiting for transfers between devices, shards(): a_even = lax.ppermute(a_even, 'row', even)  1.76 us
    ppermute x1, waiting for transfers between devices, shards(): b_even = lax.ppermute(b_even, 'row', even)  1.45 us
    ppermute x1, waiting for transfers between devices, shards(): a_odd = lax.ppermute(a_odd, 'row', odd)  1.15 us
    ppermute x1, starting transfers between devices, shards(): b_even = lax.ppermute(b_even, 'row', even)  0.92 us
  transfers between devices with their start and end apart: 4, of which 4 were waited for; matrix products, arithmetic and copies ran while one was open for 0% of the time, Pallas kernels for 35%

profile of v3, /device:TPU:6, one launch (start us, length us, event | category | flops | bytes accessed | tf_op | source)
XLA Modules:
  0.0 32.8 jit_solution(903139621836019577)
XLA Ops:
  0.6 3.0 %start.1 = (f32[124,8,128]{2,1,0:T(8,128)S(1)}, f32[124,8,128]{2,1,0:T(8,128)S(1)}, f32[2,130,24,128]{3,2,1,0:T(8,128)S(1)}, f32[2,130,8,128]{3,2,1,0:T(8,128)S(...) custom-call(f32[2,16,16384]{2,1,0:T(8,128)} %f_hbm.1, ...), custom_call_target="tpu_custom_call" | custom-call | tf_op jit(solution)/shard_map/start/pallas_call | solution.py:545
  3.6 6.5 %collective-permute-start.2 = (f32[124,8,128]{2,1,0:T(8,128)S(1)}, f32[124,8,128]{2,1,0:T(8,128)S(1)}, u32[]{:S(2)}, u32[]{:S(2)}) collective-permute-start(f32[124,8,128]{2,1,0:T(8,128)S(1)} %get-tuple-element.43), channel_id=1, source_target_pairs={{1,2},{3,4},{5,6},{7,8},{9,10},{11,12},{13,14},{15,16},{17,18},{19... | collective-permute-start | bytes 1523720 | tf_op jit(solution)/shard_map/ppermute | solution.py:591
  10.2 0.1 collective-permute-start.3
  10.3 0.8 %edge.1 = (f32[84,8,128]{2,1,0:T(8,128)S(1)}, f32[84,8,128]{2,1,0:T(8,128)S(1)}, f32[2,130,8,128]{3,2,1,0:T(8,128)S(1)}, f32[2,128,8,128]{3,2,1,0:T(8,128)S(1)}, f32[2,128,8,128]{3,2,1,0:T(8,128)S(1)}) custom-call(f32[2,130,24,128]{3,2,1,0:T(8,128)S(1)} %get-tuple-element.28.x0, ...), custom_call_target="tpu_custom_call", output_to_operand_aliasing={{2}: (2, {}), {3}: (3, {}), {4}: (4, {})} | custom-call | tf_op jit(solution)/shard_map/edge/pallas_call | solution.py:545
  11.1 3.1 %collective-permute-start = (f32[84,8,128]{2,1,0:T(8,128)S(1)}, f32[84,8,128]{2,1,0:T(8,128)S(1)}, u32[]{:S(2)}, u32[]{:S(2)}) collective-permute-start(f32[84,8,128]{2,1,0:T(8,128)S(1)} %get-tuple-element.33), channel_id=1, source_target_pairs={{1,2},{3,4},{5,6},{7,8},{9,10},{11,12},{13,14},{15,16},{17,18},{19... | collective-permute-start | bytes 1032200 | tf_op jit(solution)/shard_map/ppermute | solution.py:610
  14.2 0.9 %collective-permute-start.1 = (f32[84,8,128]{2,1,0:T(8,128)S(1)}, f32[84,8,128]{2,1,0:T(8,128)S(1)}, u32[]{:S(2)}, u32[]{:S(2)}) collective-permute-start(f32[84,8,128]{2,1,0:T(8,128)S(1)} %get-tuple-element.34), channel_id=1, source_target_pairs={{0,1},{2,3},{4,5},{6,7},{8,9},{10,11},{12,13},{14,15},{16,17},{18,... | collective-permute-start | bytes 1032200 | tf_op jit(solution)/shard_map/ppermute | solution.py:611
  15.1 6.8 %inner.1 = (f32[2,128,8,128]{3,2,1,0:T(8,128)S(1)}, f32[2,128,8,128]{3,2,1,0:T(8,128)S(1)}, f32[2,128,8,128]{3,2,1,0:T(8,128)S(1)}, f32[32,8,128]{2,1,0:T(8,128)S(1)}) custom-call(f32[2,130,24,128]{3,2,1,0:T(8,128)S(1)} %get-tuple-element.28.x0, f32[2,130,8,128]{3,2,1,0:T(8,128)S(1)} %get-tuple-element.37.f1, ...), custom_call_target="tpu_custom_call" | custom-call | tf_op jit(solution)/shard_map/inner/pallas_call | solution.py:545
  21.8 1.2 %collective-permute-done.2.a_odd.refs_0_ = f32[124,8,128]{2,1,0:T(8,128)S(1)} collective-permute-done((f32[124,8,128]{2,1,0:T(8,128)S(1)}, f32[124,8,128]{2,1,0:T(8,128)S(1)}, u32[]{:S(2)}, u32[]{:S(2)}) %collective-permute-start.2) | collective-permute-done | bytes 507936 | tf_op jit(solution)/shard_map/ppermute | solution.py:591
  23.0 1.8 %collective-permute-done.3.a_even.refs_1_ = f32[124,8,128]{2,1,0:T(8,128)S(1)} collective-permute-done((f32[124,8,128]{2,1,0:T(8,128)S(1)}, f32[124,8,128]{2,1,0:T(8,128)S(1)}, u32[]{:S(2)}, u32[]{:S(2)}) %collective-permute-start.3) | collective-permute-done | bytes 507936 | tf_op jit(solution)/shard_map/ppermute | solution.py:592
  24.8 1.2 %coarse.1 = (f32[2,4,4096]{2,1,0:T(4,128)}, f32[128,4,8,128]{3,2,1,0:T(8,128)S(1)}) custom-call(f32[32,8,128]{2,1,0:T(8,128)S(1)} %get-tuple-element.42.part, f32[124,8,128]{2,1,0:T(8,128)S(1)} %collective-permute-done.2.a_odd.refs_0_, f32[124,8,128]{2,1,0:T(8,128)S(1)} %collective-permute-done.3.a_even.refs_1_), custom_call_target="tpu_custom_call" | custom-call | tf_op jit(solution)/shard_map/coarse/pallas_call | solution.py:545
  25.9 2.7 %early.1 = (f32[2,16,16384]{2,1,0:T(8,128)}, f32[2,16,16384]{2,1,0:T(8,128)}, f32[2,2,24,128]{3,2,1,0:T(8,128)S(1)}, f32[2,2,16,128]{3,2,1,0:T(8,128)S(1)}) custom-call(f32[124,8,128]{2,1,0:T(8,128)S(1)} %collective-permute-done.2.a_odd.refs_0_, f32[124,8,128]{2,1,0:T(8,128)S(1)} %collective-permute-done.3.a_even.refs_1_, ...), custom_call_target="tpu_custom_call" | custom-call | tf_op jit(solution)/shard_map/early/pallas_call | solution.py:545
  28.6 0.6 %collective-permute-done.refs_0_ = f32[84,8,128]{2,1,0:T(8,128)S(1)} collective-permute-done((f32[84,8,128]{2,1,0:T(8,128)S(1)}, f32[84,8,128]{2,1,0:T(8,128)S(1)}, u32[]{:S(2)}, u32[]{:S(2)}) %collective-permute-start) | collective-permute-done | bytes 344096 | tf_op jit(solution)/shard_map/ppermute | solution.py:610
  29.2 1.4 %collective-permute-done.1.refs_1_ = f32[84,8,128]{2,1,0:T(8,128)S(1)} collective-permute-done((f32[84,8,128]{2,1,0:T(8,128)S(1)}, f32[84,8,128]{2,1,0:T(8,128)S(1)}, u32[]{:S(2)}, u32[]{:S(2)}) %collective-permute-start.1) | collective-permute-done | bytes 344096 | tf_op jit(solution)/shard_map/ppermute | solution.py:611
  30.7 2.2 %late.1 = (f32[2,16,16384]{2,1,0:T(8,128)}, f32[2,16,16384]{2,1,0:T(8,128)}) custom-call(f32[84,8,128]{2,1,0:T(8,128)S(1)} %collective-permute-done.refs_0_, f32[84,8,128]{2,1,0:T(8,128)S(1)} %collective-permute-done.1.refs_1_, f32[2,128,8,128]{3,2,1,0:T(8,128)S(1)} %get-tuple-element.35.refs_2_, ...), custom_call_target="tpu_custom_call", output_to_operand_aliasing={{0}: (10, {}), {1}: (11, {})} | custom-call | tf_op jit(solution)/shard_map/late/pallas_call | solution.py:545
Async XLA Ops:
  3.6 19.4 %collective-permute-start.2 = (f32[124,8,128]{2,1,0:T(8,128)S(1)}, f32[124,8,128]{2,1,0:T(8,128)S(1)}, u32[]{:S(2)}, u32[]{:S(2)}) collective-permute-start(f32[124,8,128]{2,1,0:T(8,128)S(1)} %get-tuple-element.43), channel_id=1, source_target_pairs={{1,2},{3,4},{5,6},{7,8},{9,10},{11,12},{13,14},{15,16},{17,18},{19... | collective-permute-start | bytes 1523720 | tf_op jit(solution)/shard_map/ppermute | solution.py:591
  10.2 14.6 %collective-permute-start.3 = (f32[124,8,128]{2,1,0:T(8,128)S(1)}, f32[124,8,128]{2,1,0:T(8,128)S(1)}, u32[]{:S(2)}, u32[]{:S(2)}) collective-permute-start(f32[124,8,128]{2,1,0:T(8,128)S(1)} %get-tuple-element.44), channel_id=1, source_target_pairs={{0,1},{2,3},{4,5},{6,7},{8,9},{10,11},{12,13},{14,15},{16,17},{18,... | collective-permute-start | bytes 1523720 | tf_op jit(solution)/shard_map/ppermute | solution.py:592
  11.1 18.2 %collective-permute-start = (f32[84,8,128]{2,1,0:T(8,128)S(1)}, f32[84,8,128]{2,1,0:T(8,128)S(1)}, u32[]{:S(2)}, u32[]{:S(2)}) collective-permute-start(f32[84,8,128]{2,1,0:T(8,128)S(1)} %get-tuple-element.33), channel_id=1, source_target_pairs={{1,2},{3,4},{5,6},{7,8},{9,10},{11,12},{13,14},{15,16},{17,18},{19... | collective-permute-start | bytes 1032200 | tf_op jit(solution)/shard_map/ppermute | solution.py:610
  14.2 16.5 %collective-permute-start.1 = (f32[84,8,128]{2,1,0:T(8,128)S(1)}, f32[84,8,128]{2,1,0:T(8,128)S(1)}, u32[]{:S(2)}, u32[]{:S(2)}) collective-permute-start(f32[84,8,128]{2,1,0:T(8,128)S(1)} %get-tuple-element.34), channel_id=1, source_target_pairs={{0,1},{2,3},{4,5},{6,7},{8,9},{10,11},{12,13},{14,15},{16,17},{18,... | collective-permute-start | bytes 1032200 | tf_op jit(solution)/shard_map/ppermute | solution.py:611
